TPU v7x, 128 devices: a whole 4x4x4 slice. The times are simulated.
128 devices in a mesh: vel: 4 (over y_lo, core), pos: 32 (over y_hi, z, x).
Axes of the slice: x: 4, y: 4 (y_hi: 2, y_lo: 2; y = y_hi * 2 + y_lo), z: 4, core: 2. Of those that a mesh axis runs over, the one named last changes fastest.
Arguments:
- value_next: float32 [64, 64, 64, 512], P('pos', 'vel'), may hold values from -6 to 6
- density: float32 [64, 64, 64, 512], P('pos', 'vel'), as said below
Outputs:
- value_now: float32 [64, 64, 64, 512], P('pos', 'vel')
- density_next: float32 [64, 64, 64, 512], P('pos', 'vel')
Inputs may be any that keep to these rules, and one draw needn't show every extreme that they name: density is positive everywhere.
All inputs are finite; a program needn't handle non-finite values.
Results may differ from a plain program's by a relative error of at most 0.00002.
Values sent between devices are 32-bit elements; how exact they have to be, the bound alone decides.
A program may use at most 192 MiB of HBM per device.

v0:
```python
import jax
import jax.numpy as jnp
from jax import lax
from jax.sharding import PartitionSpec as P

COURANT = 0.4
CONTROL_COST = 0.25
VISCOSITY = 0.15
CROWDING = 0.3


def from_behind(block, axis, distance):
    devices = range(lax.axis_size(axis))
    route = [((i - distance) % len(devices), i) for i in devices]
    return lax.ppermute(block, axis, route)


def passed_along(value, axis, steps):
    count = lax.axis_size(axis)
    leading, last = (max(0, -steps), min(count, count - steps))
    return lax.ppermute(value, axis, [(source, source + steps) for source in range(leading, last)])


def speeds(first, count, total):
    index = first + jnp.arange(count, dtype=jnp.int32)
    return COURANT * ((index.astype(jnp.float32) + 0.5 - total / 2) / (total / 2))


def along_second(array, step):
    rolled = jnp.roll(array, -step, 2)
    place = lax.broadcasted_iota(jnp.int32, array.shape, 2)
    edge = array.shape[2] - 1 if step > 0 else 0
    return jnp.where(place == edge, array, rolled)


def value_core(centre, x_up, x_dn, a_up, a_dn, speed_x, speed_y, crowding):
    along_x = speed_x[None, :, None, None]
    along_y = speed_y[None, None, :, None]
    carry_x = jnp.where(along_x > 0, along_x * (x_up - centre), along_x * (centre - x_dn))
    ahead_y = jnp.roll(centre, -1, 3) - centre
    behind_y = centre - jnp.roll(centre, 1, 3)
    carry_y = jnp.where(along_y > 0, along_y * ahead_y, along_y * behind_y)
    upper_v = a_up - centre
    lower_v = centre - a_dn
    upper_w = along_second(centre, 1) - centre
    lower_w = centre - along_second(centre, -1)
    hamilton = 0.5 * (
        jnp.square(jnp.maximum(lower_v, 0.0))
        + jnp.square(jnp.minimum(upper_v, 0.0))
        + jnp.square(jnp.maximum(lower_w, 0.0))
        + jnp.square(jnp.minimum(upper_w, 0.0))
    )
    laplace = upper_v - lower_v + upper_w - lower_w
    return (
        centre
        + carry_x
        + carry_y
        - CONTROL_COST * hamilton
        + VISCOSITY * laplace
        + crowding[:, None, None, :]
    )


def density_core(centre, x_up, x_dn, a_up, a_dn, control, control_up, control_dn, speed_x, speed_y):
    along_x = speed_x[None, :, None, None]
    along_y = speed_y[None, None, :, None]
    carry_x = jnp.where(along_x > 0, along_x * (centre - x_dn), along_x * (x_up - centre))
    behind_y = centre - jnp.roll(centre, 1, 3)
    ahead_y = jnp.roll(centre, -1, 3) - centre
    carry_y = jnp.where(along_y > 0, along_y * behind_y, along_y * ahead_y)
    speed_up = -CONTROL_COST * (control_up - control)
    speed_dn = -CONTROL_COST * (control - control_dn)
    flux_up = jnp.maximum(speed_up, 0.0) * centre + jnp.minimum(speed_up, 0.0) * a_up
    flux_dn = jnp.maximum(speed_dn, 0.0) * a_dn + jnp.minimum(speed_dn, 0.0) * centre
    b_up = along_second(centre, 1)
    b_dn = along_second(centre, -1)
    side_up = -CONTROL_COST * (along_second(control, 1) - control)
    side_dn = -CONTROL_COST * (control - along_second(control, -1))
    flux_right = jnp.maximum(side_up, 0.0) * centre + jnp.minimum(side_up, 0.0) * b_up
    flux_left = jnp.maximum(side_dn, 0.0) * b_dn + jnp.minimum(side_dn, 0.0) * centre
    spread = VISCOSITY * (a_up + a_dn - 2.0 * centre + b_up + b_dn - 2.0 * centre)
    return centre - carry_x - carry_y - (flux_up - flux_dn) - (flux_right - flux_left) + spread


def velocity_rows(field, from_low, from_high, bottom, summit):
    lower = jnp.concatenate([jnp.where(bottom, field[:, :1], from_low), field[:, :-1]], 1)
    upper = jnp.concatenate([field[:, 1:], jnp.where(summit, field[:, -1:], from_high)], 1)
    return (upper, lower)


def body(value_next, density):
    row_count = value_next.shape[1]
    grid_v = value_next.shape[2]
    vel_place = lax.axis_index("vel")
    vel_count = lax.axis_size("vel")
    partial_mass = jnp.sum(density, axis=(1, 2))
    mass = lax.psum(partial_mass, "vel") / (grid_v * grid_v)
    crowding = CROWDING * mass * mass
    speed_y = speeds(0, grid_v, grid_v)
    speed_x = speeds(vel_place * row_count, row_count, grid_v)
    below_value, below_density = from_behind((value_next[-1:], density[-1:]), "pos", 1)
    above_value, above_density = from_behind((value_next[:1], density[:1]), "pos", -1)
    value_x_dn = jnp.concatenate([below_value, value_next[:-1]], 0)
    value_x_up = jnp.concatenate([value_next[1:], above_value], 0)
    density_x_dn = jnp.concatenate([below_density, density[:-1]], 0)
    density_x_up = jnp.concatenate([density[1:], above_density], 0)
    bottom = vel_place == 0
    summit = vel_place == vel_count - 1
    low_value, low_density = passed_along((value_next[:, -1:], density[:, -1:]), "vel", 1)
    high_value, high_density = passed_along((value_next[:, :1], density[:, :1]), "vel", -1)
    value_a_up, value_a_dn = velocity_rows(value_next, low_value, high_value, bottom, summit)
    density_a_up, density_a_dn = velocity_rows(density, low_density, high_density, bottom, summit)
    value_now = value_core(
        value_next, value_x_up, value_x_dn, value_a_up, value_a_dn, speed_x, speed_y, crowding
    )
    low_control = passed_along(value_now[:, -1:], "vel", 1)
    high_control = passed_along(value_now[:, :1], "vel", -1)
    control_up, control_dn = velocity_rows(value_now, low_control, high_control, bottom, summit)
    density_next = density_core(
        density,
        density_x_up,
        density_x_dn,
        density_a_up,
        density_a_dn,
        value_now,
        control_up,
        control_dn,
        speed_x,
        speed_y,
    )
    return (value_now, density_next)


def solution(mesh):
    placed = (P("pos", "vel", None, None), P("pos", "vel", None, None))
    return jax.shard_map(
        body,
        mesh=mesh,
        in_specs=placed,
        out_specs=(P("pos", "vel", None, None), P("pos", "vel", None, None)),
        check_vma=False,
    )
```

profile of v0, /device:TPU:7, one launch (start us, length us, event | category | flops | bytes accessed | tf_op | source)
XLA Modules:
  0.0 188.8 jit_solution(12290915281487704804)
XLA Ops:
  2.5 3.8 %collective-permute-start.2 = (f32[2,1,64,512]{3,2,1,0:T(8,128)}, f32[2,1,64,512]{3,2,1,0:T(8,128)}, u32[]{:S(2)}, u32[]{:S(2)}) collective-permute-start(f32[2,1,64,512]{3,2,1,0:T(8,128)} %get-tuple-element.30), channel_id=1, source_target_pairs={{0,32},{32,64},{64,96},{1,33},{33,65},{65,97},{2,34},{34,66},{66,9... | collective-permute-start | bytes 786440 | tf_op jit(solution)/shard_map/ppermute | solution.py:21
  6.3 1.9 %collective-permute-start.3 = (f32[2,1,64,512]{3,2,1,0:T(8,128)}, f32[2,1,64,512]{3,2,1,0:T(8,128)}, u32[]{:S(2)}, u32[]{:S(2)}) collective-permute-start(f32[2,1,64,512]{3,2,1,0:T(8,128)} %get-tuple-element.31), channel_id=1, source_target_pairs={{32,0},{64,32},{96,64},{33,1},{65,33},{97,65},{34,2},{66,34},{98,6... | collective-permute-start | bytes 786440 | tf_op jit(solution)/shard_map/ppermute | solution.py:21
  8.2 1.9 %fusion.29 = (f32[2,1,64,512]{3,2,1,0:T(8,128)}, f32[2,1,64,512]{3,2,1,0:T(8,128)}) fusion(f32[2,16,64,512]{3,2,1,0:T(8,128)} %param.3), kind=kLoop, calls=%fused_computation.62 | loop fusion | bytes 1048576 | tf_op jit(solution)/shard_map/slice | solution.py:110
  10.1 2.3 %collective-permute-start.7 = (f32[2,1,64,512]{3,2,1,0:T(8,128)}, f32[2,1,64,512]{3,2,1,0:T(8,128)S(1)}, u32[]{:S(2)}, u32[]{:S(2)}) collective-permute-start(f32[2,1,64,512]{3,2,1,0:T(8,128)} %get-tuple-element.12), channel_id=1, source_target_pairs={{32,0},{64,32},{96,64},{33,1},{65,33},{97,65},{34,2},{66,34},{98,6... | collective-permute-start | bytes 786440 | tf_op jit(solution)/shard_map/ppermute | solution.py:21
  12.4 4.3 %fusion.43 = (f32[1,16,64,512]{3,2,1,0:T(8,128)S(1)}, f32[1,16,64,512]{3,2,1,0:T(8,128)}) fusion(f32[2,16,64,512]{3,2,1,0:T(8,128)} %param.2), kind=kLoop, calls=%fused_computation.76 | loop fusion | bytes 8388608 | tf_op jit(solution)/shard_map/slice | solution.py:104
  22.3 2.4 %fusion.36 = (f32[1,16,64,512]{3,2,1,0:T(8,128)}, f32[1,16,64,512]{3,2,1,0:T(8,128)}) fusion(f32[2,16,64,512]{3,2,1,0:T(8,128)S(1)} %copy-done), kind=kLoop, calls=%fused_computation.69 | loop fusion | bytes 8388608 | tf_op jit(solution)/shard_map/slice | solution.py:101
  24.7 4.1 %fusion.38 = (f32[2,15,64,512]{3,2,1,0:T(8,128)}, f32[2,15,64,512]{3,2,1,0:T(8,128)}) fusion(f32[2,16,64,512]{3,2,1,0:T(8,128)S(1)} %copy-done.3), kind=kLoop, calls=%fused_computation.71 | loop fusion | bytes 15728640 | tf_op jit(solution)/shard_map/slice | solution.py:86
  28.8 4.1 %fusion.28 = (f32[2,15,64,512]{3,2,1,0:T(8,128)}, f32[2,15,64,512]{3,2,1,0:T(8,128)}) fusion(f32[2,16,64,512]{3,2,1,0:T(8,128)S(1)} %copy-done), kind=kLoop, calls=%fused_computation.61 | loop fusion | bytes 15728640 | tf_op jit(solution)/shard_map/slice | solution.py:87
  32.9 4.9 %fusion.42 = (f32[2,16,64,511]{3,2,1,0:T(8,128)}, f32[2,16,64,511]{3,2,1,0:T(8,128)}) fusion(f32[2,16,64,512]{3,2,1,0:T(8,128)S(1)} %copy-done.3), kind=kLoop, calls=%fused_computation.75 | loop fusion | bytes 16744448 | tf_op jit(solution)/shard_map/jit(_roll_static)/slice | solution.py:41
  37.8 4.3 %fusion.40 = (f32[2,16,63,512]{3,2,1,0:T(8,128)}, f32[2,16,63,512]{3,2,1,0:T(8,128)}) fusion(f32[2,16,64,512]{3,2,1,0:T(8,128)S(1)} %copy-done.3), kind=kLoop, calls=%fused_computation.73 | loop fusion | bytes 16515072 | tf_op jit(solution)/shard_map/jit(_roll_static)/slice | solution.py:30
  42.0 2.5 %reduce_sum.9 = f32[2,512]{1,0:T(2,128)S(1)} reduce(f32[2,16,64,512]{3,2,1,0:T(8,128)} %param.3, f32[]{:T(128)} %constant.20.clone.1), dimensions={1,2}, to_apply=%region_0.0 | reduce | flops 1047552 | bytes 4198404 | tf_op jit(solution)/shard_map/reduce_sum | solution.py:96
  44.5 6.7 %psum.7 = f32[2,512]{1,0:T(2,128)S(1)} all-reduce(f32[2,512]{1,0:T(2,128)S(1)} %reduce_sum.9), channel_id=1, replica_groups=mesh['vel'=4,'pos'=32] {'vel'}, use_global_device_ids=true, to_apply=%region_1.0 | all-reduce | flops 1024 | bytes 8192 | tf_op jit(solution)/shard_map/psum | solution.py:97
  51.2 8.2 %fusion.34 = (f32[2,16,64,511]{3,2,1,0:T(8,128)}, f32[2,16,64,511]{3,2,1,0:T(8,128)}) fusion(f32[2,16,64,512]{3,2,1,0:T(8,128)} %param.3), kind=kLoop, calls=%fused_computation.67 | loop fusion | bytes 16744448 | tf_op jit(solution)/shard_map/jit(_roll_static)/slice | solution.py:69
  59.3 4.2 %fusion.32 = (f32[2,16,63,512]{3,2,1,0:T(8,128)}, f32[2,16,63,512]{3,2,1,0:T(8,128)}) fusion(f32[2,16,64,512]{3,2,1,0:T(8,128)S(1)} %copy-done.1), kind=kLoop, calls=%fused_computation.65 | loop fusion | bytes 16515072 | tf_op jit(solution)/shard_map/jit(_roll_static)/slice | solution.py:30
  64.1 23.2 %collective-permute-start.9 = (f32[2,1,64,512]{3,2,1,0:T(8,128)}, f32[2,1,64,512]{3,2,1,0:T(8,128)}, u32[]{:S(2)}, u32[]{:S(2)}) collective-permute-start(f32[2,1,64,512]{3,2,1,0:T(8,128)} %get-tuple-element.13), channel_id=1, source_target_pairs={{0,32},{32,64},{64,96},{1,33},{33,65},{65,97},{2,34},{34,66},{66,9... | collective-permute-start | bytes 786440 | tf_op jit(solution)/shard_map/ppermute | solution.py:21
  91.0 40.7 %collective-permute-done.9 = f32[2,1,64,512]{3,2,1,0:T(8,128)} collective-permute-done((f32[2,1,64,512]{3,2,1,0:T(8,128)}, f32[2,1,64,512]{3,2,1,0:T(8,128)}, u32[]{:S(2)}, u32[]{:S(2)}) %collective-permute-start.9) | collective-permute-done | bytes 262176 | tf_op jit(solution)/shard_map/ppermute | solution.py:21
  131.7 2.0 %broadcast_select_fusion = (f32[2,1,64,512]{3,2,1,0:T(8,128)S(1)}, f32[2,1,64,512]{3,2,1,0:T(8,128)}) fusion(f32[2,1,64,512]{3,2,1,0:T(8,128)} %copy-done.10, pred[]{:T(512)S(6)} %eq.27, f32[2,16,64,512]{3,2,1,0:T(8,128)} %param.3, f32[2,1,64,512]{3,2,1,0:T(8,128)} %collective-permute-done.9, pred[]{:T(512)S(6)} %eq.26), kind=kLoop, calls=%fused_computation.46 | loop fusion | flops 131072 | bytes 1572866 | tf_op jit(solution)/shard_map/jit(_where)/select_n | solution.py:87
  133.7 13.8 %fusion.8 = f32[2,16,64,512]{3,2,1,0:T(8,128)S(1)} fusion(f32[2,16,64,512]{3,2,1,0:T(8,128)} %param.2, f32[1,16,64,512]{3,2,1,0:T(8,128)} %collective-permute-done, f32[1,16,64,512]{3,2,1,0:T(8,128)S(1)} %get-tuple-element.42, f32[1,16,64,512]{3,2,1,0:T(8,128)} %get-tuple-element.43, f32[1,16,64,512]{3,2,1,0:T(8,128)} %collective-permute-done.1, ...), kind=kLoop, calls=%fused_computation.13 | loop fusion | flops 47185920 | bytes 41947664 | tf_op jit(solution)/shard_map/add | solution.py:55
  148.5 1.9 %collective-permute-start.6 = (f32[2,1,64,512]{3,2,1,0:T(8,128)}, f32[2,1,64,512]{3,2,1,0:T(8,128)}, u32[]{:S(2)}, u32[]{:S(2)}) collective-permute-start(f32[2,1,64,512]{3,2,1,0:T(8,128)} %get-tuple-element.6), channel_id=1, source_target_pairs={{32,0},{64,32},{96,64},{33,1},{65,33},{97,65},{34,2},{66,34},{98,6... | collective-permute-start | bytes 786440 | tf_op jit(solution)/shard_map/ppermute | solution.py:21
  150.4 4.4 %collective-permute-start.8 = (f32[2,1,64,512]{3,2,1,0:T(8,128)}, f32[2,1,64,512]{3,2,1,0:T(8,128)}, u32[]{:S(2)}, u32[]{:S(2)}) collective-permute-start(f32[2,1,64,512]{3,2,1,0:T(8,128)} %get-tuple-element.7), channel_id=1, source_target_pairs={{0,32},{32,64},{64,96},{1,33},{33,65},{65,97},{2,34},{34,66},{66,9... | collective-permute-start | bytes 786440 | tf_op jit(solution)/shard_map/ppermute | solution.py:21
  154.8 4.3 %fusion.30 = (f32[2,16,63,512]{3,2,1,0:T(8,128)}, f32[2,16,63,512]{3,2,1,0:T(8,128)}) fusion(f32[2,16,64,512]{3,2,1,0:T(8,128)S(1)} %fusion.8), kind=kLoop, calls=%fused_computation.63 | loop fusion | bytes 16515072 | tf_op jit(solution)/shard_map/jit(_roll_static)/slice | solution.py:30
  159.2 5.0 %fusion.26 = (f32[2,15,64,512]{3,2,1,0:T(8,128)}, f32[2,15,64,512]{3,2,1,0:T(8,128)}) fusion(f32[2,16,64,512]{3,2,1,0:T(8,128)S(1)} %fusion.8), kind=kLoop, calls=%fused_computation.59 | loop fusion | bytes 15728640 | tf_op jit(solution)/shard_map/slice | solution.py:87
  164.4 1.9 %broadcast_select_fusion.1 = (f32[2,1,64,512]{3,2,1,0:T(8,128)S(1)}, f32[2,1,64,512]{3,2,1,0:T(8,128)S(1)}) fusion(f32[2,1,64,512]{3,2,1,0:T(8,128)} %collective-permute-done.6, pred[]{:T(512)S(6)} %eq.27, f32[2,16,64,512]{3,2,1,0:T(8,128)S(1)} %fusion.8, f32[2,1,64,512]{3,2,1,0:T(8,128)} %collective-permute-done.8, pred[]{:T(512)S(6)} %eq.26), kind=kLoop, calls=%fused_computation.47 | loop fusion | flops 131072 | bytes 1572866 | tf_op jit(solution)/shard_map/jit(_where)/select_n | solution.py:87
  168.0 20.8 %fusion.19 = f32[2,16,64,512]{3,2,1,0:T(8,128)} fusion(f32[2,16,64,512]{3,2,1,0:T(8,128)S(1)} %copy-done.2, f32[1,16,64,512]{3,2,1,0:T(8,128)} %get-tuple-element.27, f32[1,16,64,512]{3,2,1,0:T(8,128)} %collective-permute-done.4, f32[1,16,64,512]{3,2,1,0:T(8,128)} %collective-permute-done.5, f32[1,16,64,512]{3,2,1,0:T(8,128)} %get-tuple-element.26, ...), kind=kLoop, calls=%fused_computation.30 | loop fusion | flops 71303168 | bytes 62915088 | tf_op jit(solution)/shard_map/add | solution.py:82
  (59 shorter events, 14.4 us)
Async XLA Ops:
  2.5 61.6 %collective-permute-start.2 = (f32[2,1,64,512]{3,2,1,0:T(8,128)}, f32[2,1,64,512]{3,2,1,0:T(8,128)}, u32[]{:S(2)}, u32[]{:S(2)}) collective-permute-start(f32[2,1,64,512]{3,2,1,0:T(8,128)} %get-tuple-element.30), channel_id=1, source_target_pairs={{0,32},{32,64},{64,96},{1,33},{33,65},{65,97},{2,34},{34,66},{66,9... | collective-permute-start | bytes 786440 | tf_op jit(solution)/shard_map/ppermute | solution.py:21
  6.3 81.7 %collective-permute-start.3 = (f32[2,1,64,512]{3,2,1,0:T(8,128)}, f32[2,1,64,512]{3,2,1,0:T(8,128)}, u32[]{:S(2)}, u32[]{:S(2)}) collective-permute-start(f32[2,1,64,512]{3,2,1,0:T(8,128)} %get-tuple-element.31), channel_id=1, source_target_pairs={{32,0},{64,32},{96,64},{33,1},{65,33},{97,65},{34,2},{66,34},{98,6... | collective-permute-start | bytes 786440 | tf_op jit(solution)/shard_map/ppermute | solution.py:21
  10.1 8.2 %copy-start.3 = (f32[2,16,64,512]{3,2,1,0:T(8,128)S(1)}, f32[2,16,64,512]{3,2,1,0:T(8,128)}, u32[]{:S(2)}) copy-start(f32[2,16,64,512]{3,2,1,0:T(8,128)} %param.2) | copy-start | bytes 12582916
  10.1 8.3 %copy-start = (f32[2,16,64,512]{3,2,1,0:T(8,128)S(1)}, f32[2,16,64,512]{3,2,1,0:T(8,128)}, u32[]{:S(2)}) copy-start(f32[2,16,64,512]{3,2,1,0:T(8,128)} %param.3) | copy-start | bytes 12582916
  10.1 79.1 %collective-permute-start.7 = (f32[2,1,64,512]{3,2,1,0:T(8,128)}, f32[2,1,64,512]{3,2,1,0:T(8,128)S(1)}, u32[]{:S(2)}, u32[]{:S(2)}) collective-permute-start(f32[2,1,64,512]{3,2,1,0:T(8,128)} %get-tuple-element.12), channel_id=1, source_target_pairs={{32,0},{64,32},{96,64},{33,1},{65,33},{97,65},{34,2},{66,34},{98,6... | collective-permute-start | bytes 786440 | tf_op jit(solution)/shard_map/ppermute | solution.py:21
  16.7 117.0 %collective-permute-start.1 = (f32[1,16,64,512]{3,2,1,0:T(8,128)S(1)}, f32[1,16,64,512]{3,2,1,0:T(8,128)}, u32[]{:S(2)}, u32[]{:S(2)}) collective-permute-start(f32[1,16,64,512]{3,2,1,0:T(8,128)S(1)} %get-tuple-element.42), channel_id=1, source_target_pairs={{31,0},{0,1},{1,2},{2,3},{3,4},{4,5},{5,6},{6,7},{7,8},{8,9},{9,10... | collective-permute-start | bytes 6291464 | tf_op jit(solution)/shard_map/ppermute | solution.py:15
  18.3 115.4 %collective-permute-start = (f32[1,16,64,512]{3,2,1,0:T(8,128)}, f32[1,16,64,512]{3,2,1,0:T(8,128)}, u32[]{:S(2)}, u32[]{:S(2)}) collective-permute-start(f32[1,16,64,512]{3,2,1,0:T(8,128)} %get-tuple-element.43), channel_id=1, source_target_pairs={{1,0},{2,1},{3,2},{4,3},{5,4},{6,5},{7,6},{8,7},{9,8},{10,9},{11,1... | collective-permute-start | bytes 6291464 | tf_op jit(solution)/shard_map/ppermute | solution.py:15
  51.2 8.2 %copy-start.1 = (f32[2,16,64,512]{3,2,1,0:T(8,128)S(1)}, f32[2,16,64,512]{3,2,1,0:T(8,128)}, u32[]{:S(2)}) copy-start(f32[2,16,64,512]{3,2,1,0:T(8,128)} %param.3) | copy-start | bytes 12582916
  64.1 67.6 %collective-permute-start.9 = (f32[2,1,64,512]{3,2,1,0:T(8,128)}, f32[2,1,64,512]{3,2,1,0:T(8,128)}, u32[]{:S(2)}, u32[]{:S(2)}) collective-permute-start(f32[2,1,64,512]{3,2,1,0:T(8,128)} %get-tuple-element.13), channel_id=1, source_target_pairs={{0,32},{32,64},{64,96},{1,33},{33,65},{65,97},{2,34},{34,66},{66,9... | collective-permute-start | bytes 786440 | tf_op jit(solution)/shard_map/ppermute | solution.py:21
  88.0 78.3 %collective-permute-start.4 = (f32[1,16,64,512]{3,2,1,0:T(8,128)}, f32[1,16,64,512]{3,2,1,0:T(8,128)}, u32[]{:S(2)}, u32[]{:S(2)}) collective-permute-start(f32[1,16,64,512]{3,2,1,0:T(8,128)} %get-tuple-element.26), channel_id=1, source_target_pairs={{31,0},{0,1},{1,2},{2,3},{3,4},{4,5},{5,6},{6,7},{7,8},{8,9},{9,10... | collective-permute-start | bytes 6291464 | tf_op jit(solution)/shard_map/ppermute | solution.py:15
  89.3 77.1 %collective-permute-start.5 = (f32[1,16,64,512]{3,2,1,0:T(8,128)}, f32[1,16,64,512]{3,2,1,0:T(8,128)}, u32[]{:S(2)}, u32[]{:S(2)}) collective-permute-start(f32[1,16,64,512]{3,2,1,0:T(8,128)} %get-tuple-element.27), channel_id=1, source_target_pairs={{1,0},{2,1},{3,2},{4,3},{5,4},{6,5},{7,6},{8,7},{9,8},{10,9},{11,1... | collective-permute-start | bytes 6291464 | tf_op jit(solution)/shard_map/ppermute | solution.py:15
  147.5 18.8 %copy-start.4 = (f32[2,16,64,512]{3,2,1,0:T(8,128)}, f32[2,16,64,512]{3,2,1,0:T(8,128)S(1)}, u32[]{:S(2)}) copy-start(f32[2,16,64,512]{3,2,1,0:T(8,128)S(1)} %fusion.8) | copy-start | bytes 12582916
  148.5 15.9 %collective-permute-start.6 = (f32[2,1,64,512]{3,2,1,0:T(8,128)}, f32[2,1,64,512]{3,2,1,0:T(8,128)}, u32[]{:S(2)}, u32[]{:S(2)}) collective-permute-start(f32[2,1,64,512]{3,2,1,0:T(8,128)} %get-tuple-element.6), channel_id=1, source_target_pairs={{32,0},{64,32},{96,64},{33,1},{65,33},{97,65},{34,2},{66,34},{98,6... | collective-permute-start | bytes 786440 | tf_op jit(solution)/shard_map/ppermute | solution.py:21
  150.4 14.0 %collective-permute-start.8 = (f32[2,1,64,512]{3,2,1,0:T(8,128)}, f32[2,1,64,512]{3,2,1,0:T(8,128)}, u32[]{:S(2)}, u32[]{:S(2)}) collective-permute-start(f32[2,1,64,512]{3,2,1,0:T(8,128)} %get-tuple-element.7), channel_id=1, source_target_pairs={{0,32},{32,64},{64,96},{1,33},{33,65},{65,97},{2,34},{34,66},{66,9... | collective-permute-start | bytes 786440 | tf_op jit(solution)/shard_map/ppermute | solution.py:21
  154.8 11.5 %copy-start.8 = (f32[2,16,64,1]{3,2,1,0:T(8,128)S(1)}, f32[2,16,64,1]{3,2,1,0:T(8,128)}, u32[]{:S(2)}) copy-start(f32[2,16,64,1]{3,2,1,0:T(8,128)} %get-tuple-element.24) | copy-start | bytes 24580
  159.1 7.2 %copy-start.5 = (f32[2,16,64,511]{3,2,1,0:T(8,128)S(1)}, f32[2,16,64,511]{3,2,1,0:T(8,128)}, u32[]{:S(2)}) copy-start(f32[2,16,64,511]{3,2,1,0:T(8,128)} %get-tuple-element.22) | copy-start | bytes 12558340
  159.1 7.7 %copy-start.6 = (f32[2,16,64,511]{3,2,1,0:T(8,128)S(1)}, f32[2,16,64,511]{3,2,1,0:T(8,128)}, u32[]{:S(2)}) copy-start(f32[2,16,64,511]{3,2,1,0:T(8,128)} %get-tuple-element.23) | copy-start | bytes 12558340
  159.1 8.8 %copy-start.7 = (f32[2,16,63,512]{3,2,1,0:T(8,128)S(1)}, f32[2,16,63,512]{3,2,1,0:T(8,128)}, u32[]{:S(2)}) copy-start(f32[2,16,63,512]{3,2,1,0:T(8,128)} %get-tuple-element.18) | copy-start | bytes 12386308
  159.1 8.8 %copy-start.9 = (f32[2,1,64,512]{3,2,1,0:T(8,128)S(1)}, f32[2,1,64,512]{3,2,1,0:T(8,128)}, u32[]{:S(2)}) copy-start(f32[2,1,64,512]{3,2,1,0:T(8,128)} %get-tuple-element.11) | copy-start | bytes 786436
  159.2 8.8 %copy-start.11 = (f32[2,16,1,512]{3,2,1,0:T(1,128)S(1)}, f32[2,16,1,512]{3,2,1,0:T(1,128)}, u32[]{:S(2)}) copy-start(f32[2,16,1,512]{3,2,1,0:T(1,128)} %get-tuple-element.20) | copy-start | bytes 196612
  159.2 8.8 %copy-start.12 = (f32[2,16,1,512]{3,2,1,0:T(1,128)S(1)}, f32[2,16,1,512]{3,2,1,0:T(1,128)}, u32[]{:S(2)}) copy-start(f32[2,16,1,512]{3,2,1,0:T(1,128)} %get-tuple-element.21) | copy-start | bytes 196612
  159.2 8.8 %copy-start.13 = (pred[64]{0:T(512)(128)(4,1)S(1)}, pred[64]{0:T(512)(128)(4,1)}, u32[]{:S(2)}) copy-start(pred[64]{0:T(512)(128)(4,1)} %get-tuple-element.44) | copy-start | bytes 196
  159.2 8.8 %copy-start.14 = (pred[64]{0:T(512)(128)(4,1)S(1)}, pred[64]{0:T(512)(128)(4,1)}, u32[]{:S(2)}) copy-start(pred[64]{0:T(512)(128)(4,1)} %get-tuple-element.45) | copy-start | bytes 196
  159.2 8.8 %copy-start.15 = (f32[64]{0:T(128)S(1)}, f32[64]{0:T(128)}, u32[]{:S(2)}) copy-start(f32[64]{0:T(128)} %add_multiply_fusion) | copy-start | bytes 772
  (2 other events, 8.9 us)
where the time goes:
time: 189 us
  local copies, waits for them, and re-layouts  56.2 us (30%)
  other arithmetic  43.5 us (23%)
  starting transfers between devices  40.8 us (22%)
  waiting for transfers between devices  40.8 us (22%)
  blocking collectives  6.67 us (4%)
    ppermute x6, waiting for transfers between devices, passed_along(): lax.ppermute(value, axis, [(source, source + steps) for source in range(l...  40.7 us
    ppermute x6, starting transfers between devices, passed_along(): lax.ppermute(value, axis, [(source, source + steps) for source in range(l...  37.5 us
    add x1, other arithmetic, density_core(): centre - carry_x - carry_y - (flux_up - flux_dn) - (flux_right - flux_left)  20.8 us
    add x1, other arithmetic, value_core(): centre + carry_x + carry_y - CONTROL_COST * hamilton + VISCOSITY * laplace  13.8 us
    slice x6, local copies, waits for them, and re-layouts, along_second(): rolled = jnp.roll(array, -step, 2)  13.8 us
    slice x2, local copies, waits for them, and re-layouts, density_core(): ahead_y = jnp.roll(centre, -1, 3) - centre  9.87 us
    slice x2, local copies, waits for them, and re-layouts, velocity_rows(): field[:, 1:]  9.1 us
    psum x1, blocking collectives, body(): mass = lax.psum(partial_mass, 'vel') / (grid_v * grid_v)  6.67 us
  transfers between devices with their start and end apart: 10, of which 1 were waited for; matrix products, arithmetic and copies ran while one was open for 40% of the time, Pallas kernels for 0%

commit v1 on v0

v1 whole, which is shorter than its diff:
```python
import functools

import jax
import jax.numpy as jnp
from jax import lax
from jax.experimental import pallas as pl
from jax.experimental.pallas import tpu as pltpu
from jax.sharding import PartitionSpec as P

MESH = pl.DeviceIdType.MESH
COURANT = 0.4
CROWDING = 0.3
ROWS = 16
GRID_V = 64
NY = 512
TILE = 8
TILES = GRID_V // TILE
VEL = 4
POS = 32
F32 = jnp.float32
PASSED = range(1, 8)


def tile(t):
    return pl.ds(t * TILE, TILE)


def sublane():
    return lax.broadcasted_iota(jnp.int32, (TILE, NY), 0)


def speed_b(t):
    index = (sublane() + t * TILE).astype(F32)
    return jnp.abs(COURANT * ((index + 0.5 - GRID_V / 2) / (GRID_V / 2)))


def value_slab(c_ref, up_ref, dn_ref, x_ref, crowd, speed_x, out_ref):
    place = sublane()
    c = c_ref[tile(0), :]
    turned = pltpu.roll(c, TILE - 1, 0)
    carried = jnp.zeros((TILE, NY), F32)
    for t in range(TILES):
        if t + 1 < TILES:
            c_next = c_ref[tile(t + 1), :]
            turned_next = pltpu.roll(c_next, TILE - 1, 0)
        else:
            c_next, turned_next = None, c
        upper = jnp.where(place == TILE - 1, turned_next, turned) - c
        gain = upper * (1.2 - jnp.minimum(upper, 0.0))
        loss = pltpu.roll(upper * (1.2 + jnp.maximum(upper, 0.0)), 1, 0)
        gain = gain - jnp.where(place == 0, carried, loss)
        carried = loss
        a_upper = up_ref[tile(t), :] - c
        a_lower = c - dn_ref[tile(t), :]
        gain = gain + a_upper * (1.2 - jnp.minimum(a_upper, 0.0))
        gain = gain - a_lower * (1.2 + jnp.maximum(a_lower, 0.0))
        y_next = pltpu.roll(c, 1 if t < TILES // 2 else NY - 1, 1)
        speed_y = speed_b(t)
        out = (1.0 - speed_x - speed_y) * c + speed_x * x_ref[tile(t), :] + speed_y * y_next
        out_ref[tile(t), :] = out + (0.125 * gain + crowd)
        c, turned = c_next, turned_next


def density_slab(n_ref, n_up_ref, n_dn_ref, d_ref, d_up_ref, d_dn_ref, x_ref, speed_x, out_ref):
    place = sublane()
    d, n = d_ref[tile(0), :], n_ref[tile(0), :]
    d_turned, n_turned = pltpu.roll(d, TILE - 1, 0), pltpu.roll(n, TILE - 1, 0)
    carried = jnp.zeros((TILE, NY), F32)
    for t in range(TILES):
        if t + 1 < TILES:
            d_next, n_next = d_ref[tile(t + 1), :], n_ref[tile(t + 1), :]
            d_turned_next = pltpu.roll(d_next, TILE - 1, 0)
            n_turned_next = pltpu.roll(n_next, TILE - 1, 0)
        else:
            d_next, n_next, d_turned_next, n_turned_next = None, None, d, n
        last = place == TILE - 1
        d_beyond = jnp.where(last, d_turned_next, d_turned)
        step = n - jnp.where(last, n_turned_next, n_turned)
        flux = (jnp.maximum(step, 0.0) + 0.6) * (d - d_beyond) + step * d_beyond
        turned = pltpu.roll(flux, 1, 0)
        total = jnp.where(place == 0, carried, turned) - flux
        carried = turned
        d_up, d_dn = d_up_ref[tile(t), :], d_dn_ref[tile(t), :]
        step = n - n_up_ref[tile(t), :]
        total = total - ((jnp.maximum(step, 0.0) + 0.6) * (d - d_up) + step * d_up)
        step = n_dn_ref[tile(t), :] - n
        total = total + ((jnp.maximum(step, 0.0) + 0.6) * (d_dn - d) + step * d)
        y_next = pltpu.roll(d, NY - 1 if t < TILES // 2 else 1, 1)
        speed_y = speed_b(t)
        out = (1.0 - speed_x - speed_y) * d + speed_y * y_next
        if x_ref is not None:
            out = out + speed_x * x_ref[tile(t), :]
        out_ref[tile(t), :] = out + 0.25 * total
        d, n, d_turned, n_turned = d_next, n_next, d_turned_next, n_turned_next


def kernel(
    value, density, value_out, density_out,
    v, d, hv, hd, n, dn, mass, crowd, passing,
    load_sem, edge_send, edge_recv, mass_send, mass_recv, x_send, x_recv, pass_send, pass_recv, out_sem,
):
    vel, pos = lax.axis_index("vel"), lax.axis_index("pos")
    above, below = lax.rem(pos + 1, POS), lax.rem(pos + POS - 1, POS)
    low = vel < VEL // 2
    value_to = jnp.where(low, above, below)
    density_to = jnp.where(low, below, above)
    near = jnp.where(low, 0, 1)
    far = 1 - near
    has_lower, has_upper = vel > 0, vel < VEL - 1
    half = POS // 2
    place_x = lax.rem(pos, half)
    bottom, top = place_x == 0, place_x == half - 1
    at_end = jnp.logical_or(bottom, top)
    twin = lax.rem(pos + half, POS)
    other_end = jnp.where(bottom, pos + half - 1, pos - half + 1)
    high = jnp.logical_not(low)
    value_long = jnp.logical_or(jnp.logical_and(top, low), jnp.logical_and(bottom, high))
    density_long = jnp.logical_and(at_end, jnp.logical_not(value_long))

    barrier = pltpu.get_barrier_semaphore()
    for other in (above, below):
        pl.semaphore_signal(barrier, inc=1, device_id={"pos": other}, device_id_type=MESH)
    for k in range(1, VEL):
        pl.semaphore_signal(barrier, inc=1, device_id={"vel": lax.rem(vel + k, VEL)}, device_id_type=MESH)

    @pl.when(at_end)
    def _():
        pl.semaphore_signal(barrier, inc=1, device_id={"pos": twin}, device_id_type=MESH)
        pl.semaphore_signal(barrier, inc=1, device_id={"pos": other_end}, device_id_type=MESH)

    load_d = pltpu.make_async_copy(density, d.at[:, pl.ds(1, ROWS)], load_sem.at[0])
    load_v = pltpu.make_async_copy(value, v.at[:, pl.ds(1, ROWS)], load_sem.at[1])
    load_d.start()
    load_v.start()
    pl.semaphore_wait(barrier, jnp.where(at_end, 2 + VEL - 1 + 2, 2 + VEL - 1))

    def x_copies(a):
        one = pl.ds(a, 1)
        return (
            pltpu.make_async_remote_copy(
                value.at[far, one], hv.at[one], x_send.at[0, a], x_recv.at[0, a],
                device_id={"pos": value_to}, device_id_type=MESH),
            pltpu.make_async_remote_copy(
                density.at[near, one], hd.at[one], x_send.at[1, a], x_recv.at[1, a],
                device_id={"pos": density_to}, device_id_type=MESH),
        )

    def start_x(a):
        for copy in x_copies(a):
            copy.start()

    def start_x_passed(a):
        one, k = pl.ds(a, 1), a - PASSED[0]
        for kind, (copy, source, row, crosses) in enumerate(
            zip(x_copies(a), (value, density), (far, near), (value_long, density_long))
        ):
            first_leg = pltpu.make_async_remote_copy(
                source.at[row, one], passing.at[pl.ds(k, 1)], x_send.at[kind, a], pass_recv.at[k],
                device_id={"pos": other_end}, device_id_type=MESH)
            pl.when(crosses)(first_leg.start)
            pl.when(jnp.logical_not(crosses))(copy.start)

    def second_legs(a):
        one, k = pl.ds(a, 1), a - PASSED[0]
        return [
            pltpu.make_async_remote_copy(
                passing.at[pl.ds(k, 1)], halo.at[one], pass_send.at[k], x_recv.at[kind, a],
                device_id={"pos": twin}, device_id_type=MESH)
            for kind, halo in enumerate((hv, hd))
        ]

    def pass_on(a):
        @pl.when(at_end)
        def _():
            value_leg, density_leg = second_legs(a)
            k = a - PASSED[0]
            first_leg = pltpu.make_async_remote_copy(
                value.at[far, pl.ds(a, 1)], passing.at[pl.ds(k, 1)], x_send.at[0, a], pass_recv.at[k],
                device_id={"pos": other_end}, device_id_type=MESH)
            first_leg.wait_recv()
            pl.when(density_long)(value_leg.start)
            pl.when(value_long)(density_leg.start)

    def edge_copies(k, source, target):
        to_upper = pltpu.make_async_remote_copy(
            source.at[:, pl.ds(ROWS - 1, 1)], target.at[:, pl.ds(0, 1)], edge_send.at[k, 0], edge_recv.at[k, 0],
            device_id={"vel": lax.rem(vel + 1, VEL)}, device_id_type=MESH)
        to_lower = pltpu.make_async_remote_copy(
            source.at[:, pl.ds(0, 1)], target.at[:, pl.ds(ROWS + 1, 1)], edge_send.at[k, 1], edge_recv.at[k, 1],
            device_id={"vel": lax.rem(vel + VEL - 1, VEL)}, device_id_type=MESH)
        return to_upper, to_lower

    def start_pair(pair):
        to_upper, to_lower = pair

        @pl.when(has_upper)
        def _():
            to_upper.start()

        @pl.when(has_lower)
        def _():
            to_lower.start()

    def receive_pair(pair):
        to_upper, to_lower = pair

        @pl.when(has_lower)
        def _():
            to_upper.wait_recv()

        @pl.when(has_upper)
        def _():
            to_lower.wait_recv()

    def sent_pair(pair):
        to_upper, to_lower = pair

        @pl.when(has_upper)
        def _():
            to_upper.wait_send()

        @pl.when(has_lower)
        def _():
            to_lower.wait_send()

    edges_v, edges_d = edge_copies(0, value, v), edge_copies(1, density, d)
    start_x(0)
    start_pair(edges_v)
    start_x(ROWS - 1)
    start_pair(edges_d)
    for a in range(1, ROWS - 1):
        (start_x_passed if a in PASSED else start_x)(a)

    load_d.wait()
    place = sublane()

    def add_row(i, sums):
        parts = []
        for r in range(2):
            total = sums[r]
            for t in range(TILES):
                total = total + d[r, i + 1, tile(t), :]
            parts.append(total)
        return tuple(parts)

    zero = jnp.zeros((TILE, NY), F32)
    sums = lax.fori_loop(0, ROWS, add_row, (zero, zero))
    sums = [jnp.sum(s, axis=0, keepdims=True) for s in sums]
    mass[vel] = jnp.where(place == 0, sums[0], sums[1])
    mass_copies = [
        pltpu.make_async_remote_copy(
            mass.at[vel], mass.at[vel], mass_send.at[k], mass_recv.at[k],
            device_id={"vel": lax.rem(vel + k, VEL)}, device_id_type=MESH)
        for k in range(1, VEL)
    ]
    for copy in mass_copies:
        copy.start()
    load_v.wait()

    def repeat_edges(field, rows):
        @pl.when(jnp.logical_not(has_lower))
        def _():
            for r in rows:
                field[r, 0] = field[r, 1]

        @pl.when(jnp.logical_not(has_upper))
        def _():
            for r in rows:
                field[r, ROWS + 1] = field[r, ROWS]

    repeat_edges(v, (0, 1))
    repeat_edges(d, (0, 1))
    for copy in mass_copies:
        copy.wait_recv()
    total = (mass[0] + mass[1]) + (mass[2] + mass[3])
    total = total / (GRID_V * GRID_V)
    total = CROWDING * total * total
    crowd[0] = jnp.broadcast_to(total[0:1], (TILE, NY))
    crowd[1] = jnp.broadcast_to(total[1:2], (TILE, NY))

    def speed_a(a):
        index = (vel * ROWS + a).astype(F32)
        return jnp.abs(COURANT * ((index + 0.5 - GRID_V / 2) / (GRID_V / 2)))

    def value_row(row, a, x_ref):
        value_slab(v.at[row, a + 1], v.at[row, a + 2], v.at[row, a], x_ref, crowd[row], speed_a(a), n.at[row, a + 1])

    def density_row(row, a, x_ref, out_ref):
        density_slab(
            n.at[row, a + 1], n.at[row, a + 2], n.at[row, a],
            d.at[row, a + 1], d.at[row, a + 2], d.at[row, a], x_ref, speed_a(a), out_ref)

    def write(k, row, a):
        source, target = ((n, value_out), (dn, density_out))[k]
        at = a + 1 if k == 0 else a
        return pltpu.make_async_copy(source.at[row, pl.ds(at, 1)], target.at[row, pl.ds(a, 1)], out_sem.at[k])

    def arrive(a):
        for copy in x_copies(a):
            copy.wait_recv()

    def finish_far(a):
        speed_x = speed_a(a)
        for t in range(TILES):
            dn[far, a, tile(t), :] = dn[far, a, tile(t), :] + speed_x * hd[a, tile(t), :]
        write(1, far, a).start()

    def near_density(a):
        density_row(near, a, d.at[far, a + 1], dn.at[near, a])
        write(1, near, a).start()

    @pl.loop(1, ROWS - 1)
    def _(a):
        value_row(far, a, v.at[near, a + 1])
        write(0, far, a).start()

    receive_pair(edges_v)

    @pl.loop(0, 2)
    def _(i):
        a = i * (ROWS - 1)
        arrive(a)
        value_row(far, a, v.at[near, a + 1])
        value_row(near, a, hv.at[a])
        write(0, far, a).start()
        write(0, near, a).start()

    edges_n = edge_copies(2, n.at[:, pl.ds(1, ROWS)], n)
    start_pair(edges_n)
    repeat_edges(n, (0, 1))

    @pl.loop(1, ROWS - 1)
    def _(a):
        density_row(far, a, None, dn.at[far, a])

    receive_pair(edges_d)

    pass_on(1)
    pass_on(2)
    pass_on(3)

    def near_step(a):
        arrive(a)
        value_row(near, a, hv.at[a])
        write(0, near, a).start()
        finish_far(a)

    @pl.loop(1, ROWS // 2)
    def _(a):
        pl.when(a + 3 < ROWS // 2)(lambda: pass_on(a + 3))
        near_step(a)

        @pl.when(a > 1)
        def _():
            near_density(a - 1)

    receive_pair(edges_n)

    @pl.loop(0, 2)
    def _(i):
        a = i * (ROWS - 1)
        density_row(far, a, None, dn.at[far, a])
        finish_far(a)

    near_density(0)

    @pl.loop(ROWS // 2, ROWS - 1)
    def _(a):
        near_step(a)
        near_density(a - 1)

    near_density(ROWS - 2)
    near_density(ROWS - 1)

    for pair in (edges_v, edges_d, edges_n):
        sent_pair(pair)
    for copy in mass_copies:
        copy.wait_send()

    @pl.loop(0, ROWS)
    def _(a):
        for copy in x_copies(a):
            copy.wait_send()

    @pl.when(at_end)
    def _():
        for a in PASSED:
            second_legs(a)[0].wait_send()

    pltpu.make_async_copy(n.at[:, pl.ds(1, ROWS)], value_out, out_sem.at[0]).wait()
    pltpu.make_async_copy(dn, density_out, out_sem.at[1]).wait()


def body(value_next, density):
    shape = (2, ROWS, GRID_V, NY)
    haloed = pltpu.VMEM((2, ROWS + 2, GRID_V, NY), F32)
    slab = pltpu.VMEM((ROWS, GRID_V, NY), F32)
    dma = pltpu.SemaphoreType.DMA
    return pl.pallas_call(
        kernel,
        out_shape=[jax.ShapeDtypeStruct(shape, F32)] * 2,
        in_specs=[pl.BlockSpec(memory_space=pl.ANY)] * 2,
        out_specs=[pl.BlockSpec(memory_space=pl.ANY)] * 2,
        scratch_shapes=[
            haloed, haloed, slab, slab, haloed, pltpu.VMEM(shape, F32),
            pltpu.VMEM((VEL, TILE, NY), F32), pltpu.VMEM((2, TILE, NY), F32),
            pltpu.VMEM((len(PASSED), GRID_V, NY), F32),
            dma((2,)), dma((3, 2)), dma((3, 2)), dma((VEL,)), dma((VEL,)),
            dma((2, ROWS)), dma((2, ROWS)), dma((len(PASSED),)), dma((len(PASSED),)), dma((2,)),
        ],
        compiler_params=pltpu.CompilerParams(
            collective_id=0, has_side_effects=True, vmem_limit_bytes=48 << 20
        ),
    )(value_next, density)


def solution(mesh):
    spec = P("pos", "vel", None, None)
    return jax.shard_map(body, mesh=mesh, in_specs=(spec, spec), out_specs=(spec, spec), check_vma=False)
```

time: 189 us -> 67.1 us (0.36)
  the two profiles are of different devices: /device:TPU:7 before, /device:TPU:1 now
where the time goes in v1:
time: 67.1 us; the launch traced here: 67 us
  Pallas kernels  60.6 us (90%)
  local copies, waits for them, and re-layouts  5.71 us (9%)
    pallas_call x1, Pallas kernels, body(): pl.pallas_call(kernel, out_shape=[jax.ShapeDtypeStruct(shape, F32)] * 2,...  60.6 us
    unnamed x4, local copies, waits for them, and re-layouts  5.71 us

profile of v1, /device:TPU:1, one launch (start us, length us, event | category | flops | bytes accessed | tf_op | source)
XLA Modules:
  0.0 67.0 jit_solution(6508700602975374735)
XLA Ops:
  0.6 60.6 %shard_map.41 = (f32[2,16,64,512]{3,2,1,0:T(8,128)S(1)}, f32[2,16,64,512]{3,2,1,0:T(8,128)}) custom-call(f32[2,16,64,512]{3,2,1,0:T(8,128)} %value.1, f32[2,16,64,512]{3,2,1,0:T(8,128)} %density.1), custom_call_target="tpu_custom_call" | custom-call | tf_op jit(solution)/shard_map/pallas_call | solution.py:399
  61.2 0.0 copy-start
  61.2 2.1 %copy.6 = f32[2,16,64,512]{3,2,1,0:T(8,128)} copy(f32[2,16,64,512]{3,2,1,0:T(8,128)S(1)} %get-tuple-element.4) | data formatting | bytes 8388608
  63.4 1.6 %copy-done = f32[2,16,64,512]{3,2,1,0:T(8,128)S(1)} copy-done((f32[2,16,64,512]{3,2,1,0:T(8,128)S(1)}, f32[2,16,64,512]{3,2,1,0:T(8,128)}, u32[]{:S(2)}) %copy-start) | copy-done | bytes 4194328
  64.9 2.0 %copy.7 = f32[2,16,64,512]{3,2,1,0:T(8,128)} copy(f32[2,16,64,512]{3,2,1,0:T(8,128)S(1)} %copy-done) | data formatting | bytes 8388608
Async XLA Ops:
  61.2 3.7 %copy-start = (f32[2,16,64,512]{3,2,1,0:T(8,128)S(1)}, f32[2,16,64,512]{3,2,1,0:T(8,128)}, u32[]{:S(2)}) copy-start(f32[2,16,64,512]{3,2,1,0:T(8,128)} %get-tuple-element.5) | copy-start | bytes 12582916

commit v2 on v1

v2 whole, which is shorter than its diff:
```python
import functools

import jax
import jax.numpy as jnp
from jax import lax
from jax.experimental import pallas as pl
from jax.experimental.pallas import tpu as pltpu
from jax.sharding import PartitionSpec as P

MESH = pl.DeviceIdType.MESH
COURANT = 0.4
CROWDING = 0.3
ROWS = 16
GRID_V = 64
NY = 512
TILE = 8
TILES = GRID_V // TILE
VEL = 4
POS = 32
F32 = jnp.float32
PASSED = range(1, 7)

LAST = ROWS - 2
ORDER = (1, 2, 3, 0, ROWS - 1, *range(4, ROWS - 1))


def tile(t):
    return pl.ds(t * TILE, TILE)


def sublane():
    return lax.broadcasted_iota(jnp.int32, (TILE, NY), 0)


def speed_b(t):
    index = (sublane() + t * TILE).astype(F32)
    return jnp.abs(COURANT * ((index + 0.5 - GRID_V / 2) / (GRID_V / 2)))


def value_slab(c_ref, up_ref, dn_ref, x_ref, crowd, speed_x, out_ref, first=0, stop=TILES):
    place = sublane()

    def ahead(t):
        c = c_ref[tile(t), :]
        return c, pltpu.roll(c, TILE - 1, 0)

    begin = max(first - 1, 0)
    c, turned = ahead(begin)
    carried = jnp.zeros((TILE, NY), F32)
    for t in range(begin, stop):
        c_next, turned_next = ahead(t + 1) if t + 1 < TILES else (None, c)
        upper = jnp.where(place == TILE - 1, turned_next, turned) - c
        loss = pltpu.roll(upper * (1.2 + jnp.maximum(upper, 0.0)), 1, 0)
        if t >= first:
            gain = upper * (1.2 - jnp.minimum(upper, 0.0)) - jnp.where(place == 0, carried, loss)
            a_upper = up_ref[tile(t), :] - c
            a_lower = c - dn_ref[tile(t), :]
            gain = gain + a_upper * (1.2 - jnp.minimum(a_upper, 0.0))
            gain = gain - a_lower * (1.2 + jnp.maximum(a_lower, 0.0))
            y_next = pltpu.roll(c, 1 if t < TILES // 2 else NY - 1, 1)
            speed_y = speed_b(t)
            out = (1.0 - speed_x - speed_y) * c + speed_x * x_ref[tile(t), :] + speed_y * y_next
            out_ref[tile(t), :] = out + (0.125 * gain + crowd)
        carried = loss
        c, turned = c_next, turned_next


def density_slab(n_ref, n_up_ref, n_dn_ref, d_ref, d_up_ref, d_dn_ref, x_ref, speed_x, out_ref, first=0, stop=TILES):
    place = sublane()

    def ahead(t):
        d, n = d_ref[tile(t), :], n_ref[tile(t), :]
        return d, n, pltpu.roll(d, TILE - 1, 0), pltpu.roll(n, TILE - 1, 0)

    begin = max(first - 1, 0)
    d, n, d_turned, n_turned = ahead(begin)
    carried = jnp.zeros((TILE, NY), F32)
    for t in range(begin, stop):
        d_next, n_next, d_turned_next, n_turned_next = ahead(t + 1) if t + 1 < TILES else (None, None, d, n)
        last = place == TILE - 1
        d_beyond = jnp.where(last, d_turned_next, d_turned)
        step = n - jnp.where(last, n_turned_next, n_turned)
        flux = (jnp.maximum(step, 0.0) + 0.6) * (d - d_beyond) + step * d_beyond
        turned = pltpu.roll(flux, 1, 0)
        if t >= first:
            total = jnp.where(place == 0, carried, turned) - flux
            d_up, d_dn = d_up_ref[tile(t), :], d_dn_ref[tile(t), :]
            step = n - n_up_ref[tile(t), :]
            total = total - ((jnp.maximum(step, 0.0) + 0.6) * (d - d_up) + step * d_up)
            step = n_dn_ref[tile(t), :] - n
            total = total + ((jnp.maximum(step, 0.0) + 0.6) * (d_dn - d) + step * d)
            y_next = pltpu.roll(d, NY - 1 if t < TILES // 2 else 1, 1)
            speed_y = speed_b(t)
            out = (1.0 - speed_x - speed_y) * d + speed_y * y_next
            if x_ref is not None:
                out = out + speed_x * x_ref[tile(t), :]
            out_ref[tile(t), :] = out + 0.25 * total
        carried = turned
        d, n, d_turned, n_turned = d_next, n_next, d_turned_next, n_turned_next


def kernel(
    value, density, n, dn,
    v, d, hv, hd, mass, crowd, passing,
    load_sem, edge_send, edge_recv, mass_send, mass_recv, x_send, x_recv, pass_send, pass_recv,
):
    vel, pos = lax.axis_index("vel"), lax.axis_index("pos")
    above, below = lax.rem(pos + 1, POS), lax.rem(pos + POS - 1, POS)
    low = vel < VEL // 2
    value_to = jnp.where(low, above, below)
    density_to = jnp.where(low, below, above)
    near = jnp.where(low, 0, 1)
    far = 1 - near
    has_lower, has_upper = vel > 0, vel < VEL - 1
    half = POS // 2
    place_x = lax.rem(pos, half)
    bottom, top = place_x == 0, place_x == half - 1
    at_end = jnp.logical_or(bottom, top)
    twin = lax.rem(pos + half, POS)
    other_end = jnp.where(bottom, pos + half - 1, pos - half + 1)
    high = jnp.logical_not(low)
    value_long = jnp.logical_or(jnp.logical_and(top, low), jnp.logical_and(bottom, high))
    density_long = jnp.logical_and(at_end, jnp.logical_not(value_long))

    barrier = pltpu.get_barrier_semaphore()
    for other in (above, below):
        pl.semaphore_signal(barrier, inc=1, device_id={"pos": other}, device_id_type=MESH)
    for k in range(1, VEL):
        pl.semaphore_signal(barrier, inc=1, device_id={"vel": lax.rem(vel + k, VEL)}, device_id_type=MESH)

    @pl.when(at_end)
    def _():
        pl.semaphore_signal(barrier, inc=1, device_id={"pos": twin}, device_id_type=MESH)
        pl.semaphore_signal(barrier, inc=1, device_id={"pos": other_end}, device_id_type=MESH)

    load_d = pltpu.make_async_copy(density, d.at[:, pl.ds(1, ROWS)], load_sem.at[0])
    load_v = pltpu.make_async_copy(value, v.at[:, pl.ds(1, ROWS)], load_sem.at[1])
    pl.semaphore_wait(barrier, jnp.where(at_end, 2 + VEL - 1 + 2, 2 + VEL - 1))

    def x_copies(a):
        one = pl.ds(a, 1)
        return (
            pltpu.make_async_remote_copy(
                value.at[far, one], hv.at[one], x_send.at[0, a], x_recv.at[0, a],
                device_id={"pos": value_to}, device_id_type=MESH),
            pltpu.make_async_remote_copy(
                density.at[near, one], hd.at[one], x_send.at[1, a], x_recv.at[1, a],
                device_id={"pos": density_to}, device_id_type=MESH),
        )

    def x_halves(half):
        part = pl.ds(half * (GRID_V // 2), GRID_V // 2)
        return [
            pltpu.make_async_remote_copy(
                source.at[row, LAST, part], target.at[LAST, part], x_send.at[kind, LAST + 2 * half],
                x_recv.at[kind, LAST + 2 * half], device_id={"pos": to}, device_id_type=MESH)
            for kind, (source, row, target, to) in enumerate(
                ((value, far, hv, value_to), (density, near, hd, density_to)))
        ]

    def start_x(a):
        for copy in x_halves(0) + x_halves(1) if a == LAST else x_copies(a):
            copy.start()

    def start_x_passed(a):
        one, k = pl.ds(a, 1), a - PASSED[0]
        for kind, (copy, source, row, crosses) in enumerate(
            zip(x_copies(a), (value, density), (far, near), (value_long, density_long))
        ):
            first_leg = pltpu.make_async_remote_copy(
                source.at[row, one], passing.at[pl.ds(k, 1)], x_send.at[kind, a], pass_recv.at[k],
                device_id={"pos": other_end}, device_id_type=MESH)
            pl.when(crosses)(first_leg.start)
            pl.when(jnp.logical_not(crosses))(copy.start)

    def second_leg(kind, a):
        k = a - PASSED[0]
        return pltpu.make_async_remote_copy(
            passing.at[pl.ds(k, 1)], (hv, hd)[kind].at[pl.ds(a, 1)], pass_send.at[k], x_recv.at[kind, a],
            device_id={"pos": twin}, device_id_type=MESH)

    def pass_on(a):
        @pl.when(at_end)
        def _():
            k = a - PASSED[0]
            first_leg = pltpu.make_async_remote_copy(
                value.at[far, pl.ds(a, 1)], passing.at[pl.ds(k, 1)], x_send.at[0, a], pass_recv.at[k],
                device_id={"pos": other_end}, device_id_type=MESH)
            first_leg.wait_recv()
            pl.when(density_long)(lambda: second_leg(0, a).start())
            pl.when(value_long)(lambda: second_leg(1, a).start())

    def edge_copies(k, source, target):
        to_upper = pltpu.make_async_remote_copy(
            source.at[:, pl.ds(ROWS - 1, 1)], target.at[:, pl.ds(0, 1)], edge_send.at[k, 0], edge_recv.at[k, 0],
            device_id={"vel": lax.rem(vel + 1, VEL)}, device_id_type=MESH)
        to_lower = pltpu.make_async_remote_copy(
            source.at[:, pl.ds(0, 1)], target.at[:, pl.ds(ROWS + 1, 1)], edge_send.at[k, 1], edge_recv.at[k, 1],
            device_id={"vel": lax.rem(vel + VEL - 1, VEL)}, device_id_type=MESH)
        return to_upper, to_lower

    def start_pair(pair):
        to_upper, to_lower = pair

        @pl.when(has_upper)
        def _():
            to_upper.start()

        @pl.when(has_lower)
        def _():
            to_lower.start()

    def receive_pair(pair):
        to_upper, to_lower = pair

        @pl.when(has_lower)
        def _():
            to_upper.wait_recv()

        @pl.when(has_upper)
        def _():
            to_lower.wait_recv()

    def sent_pair(pair):
        to_upper, to_lower = pair

        @pl.when(has_upper)
        def _():
            to_upper.wait_send()

        @pl.when(has_lower)
        def _():
            to_lower.wait_send()

    edges_v, edges_d = edge_copies(0, value, v), edge_copies(1, density, d)
    for a in ORDER:
        (start_x_passed if a in PASSED else start_x)(a)
        if a == ORDER[0]:
            start_pair(edges_v)
            load_d.start()
            load_v.start()
        if a == ORDER[1]:
            start_pair(edges_d)

    load_d.wait()
    place = sublane()

    def add_row(i, sums):
        parts = []
        for r in range(2):
            total = sums[r]
            for t in range(TILES):
                total = total + d[r, i + 1, tile(t), :]
            parts.append(total)
        return tuple(parts)

    zero = jnp.zeros((TILE, NY), F32)
    sums = lax.fori_loop(0, ROWS, add_row, (zero, zero))
    sums = [jnp.sum(s, axis=0, keepdims=True) for s in sums]
    mass[vel] = jnp.where(place == 0, sums[0], sums[1])
    mass_copies = [
        pltpu.make_async_remote_copy(
            mass.at[vel], mass.at[vel], mass_send.at[k], mass_recv.at[k],
            device_id={"vel": lax.rem(vel + k, VEL)}, device_id_type=MESH)
        for k in range(1, VEL)
    ]
    for copy in mass_copies:
        copy.start()
    load_v.wait()

    def repeat_edges(field, rows):
        @pl.when(jnp.logical_not(has_lower))
        def _():
            for r in rows:
                field[r, 0] = field[r, 1]

        @pl.when(jnp.logical_not(has_upper))
        def _():
            for r in rows:
                field[r, ROWS + 1] = field[r, ROWS]

    repeat_edges(v, (0, 1))
    repeat_edges(d, (0, 1))
    for copy in mass_copies:
        copy.wait_recv()
    total = (mass[0] + mass[1]) + (mass[2] + mass[3])
    total = total / (GRID_V * GRID_V)
    total = CROWDING * total * total
    crowd[0] = jnp.broadcast_to(total[0:1], (TILE, NY))
    crowd[1] = jnp.broadcast_to(total[1:2], (TILE, NY))

    def speed_a(a):
        index = (vel * ROWS + a).astype(F32)
        return jnp.abs(COURANT * ((index + 0.5 - GRID_V / 2) / (GRID_V / 2)))

    def value_row(row, a, x_ref, **tiles):
        value_slab(v.at[row, a + 1], v.at[row, a + 2], v.at[row, a], x_ref, crowd[row], speed_a(a), n.at[row, a + 1], **tiles)

    def density_row(row, a, x_ref, out_ref, **tiles):
        density_slab(
            n.at[row, a + 1], n.at[row, a + 2], n.at[row, a],
            d.at[row, a + 1], d.at[row, a + 2], d.at[row, a], x_ref, speed_a(a), out_ref, **tiles)

    def arrive(a):
        for copy in x_copies(a):
            copy.wait_recv()

    def finish_far(a, first=0, stop=TILES):
        speed_x = speed_a(a)
        for t in range(first, stop):
            dn[far, a, tile(t), :] = dn[far, a, tile(t), :] + speed_x * hd[a, tile(t), :]

    def near_density(a, **tiles):
        density_row(near, a, d.at[far, a + 1], dn.at[near, a], **tiles)

    @pl.loop(1, ROWS - 1)
    def _(a):
        value_row(far, a, v.at[near, a + 1])

    @pl.loop(2, ROWS - 2)
    def _(a):
        density_row(far, a, None, dn.at[far, a])

    receive_pair(edges_v)

    @pl.loop(0, 2)
    def _(i):
        a = i * (ROWS - 1)
        arrive(a)
        value_row(far, a, v.at[near, a + 1])
        value_row(near, a, hv.at[a])

    edges_n = edge_copies(2, n.at[:, pl.ds(1, ROWS)], n)
    start_pair(edges_n)
    repeat_edges(n, (0, 1))
    pass_on(1)
    pass_on(2)
    pass_on(3)
    pass_on(4)
    pass_on(5)
    pass_on(6)

    @pl.loop(0, 2)
    def _(i):
        a = 1 + i * (ROWS - 3)
        density_row(far, a, None, dn.at[far, a])

    receive_pair(edges_d)


    def near_step(a):
        arrive(a)
        value_row(near, a, hv.at[a])
        finish_far(a)

    @pl.loop(1, ROWS // 2)
    def _(a):
        near_step(a)

        @pl.when(a > 1)
        def _():
            near_density(a - 1)

    receive_pair(edges_n)

    @pl.loop(0, 2)
    def _(i):
        a = i * (ROWS - 1)
        density_row(far, a, None, dn.at[far, a])
        finish_far(a)

    near_density(0)

    @pl.loop(ROWS // 2, LAST)
    def _(a):
        near_step(a)
        near_density(a - 1)

    middle = TILES // 2
    for half, (first, stop, inner_first, inner_stop) in enumerate(
        ((0, middle, 0, middle - 1), (middle, TILES, middle - 1, TILES))
    ):
        for copy in x_halves(half):
            copy.wait_recv()
        value_row(near, LAST, hv.at[LAST], first=first, stop=stop)
        finish_far(LAST, first, stop)
        near_density(LAST - 1, first=first, stop=stop)
        near_density(LAST, first=inner_first, stop=inner_stop)
        near_density(LAST + 1, first=first, stop=stop)

    for pair in (edges_v, edges_d, edges_n):
        sent_pair(pair)
    for copy in mass_copies:
        copy.wait_send()

    @pl.loop(0, LAST)
    def _(a):
        for copy in x_copies(a):
            copy.wait_send()

    for copy in x_copies(ROWS - 1) + tuple(x_halves(0) + x_halves(1)):
        copy.wait_send()

    @pl.when(at_end)
    def _():
        for a in PASSED:
            second_leg(0, a).wait_send()


def store(n, dn, value_out, density_out, sem):
    copies = []
    for k, (source, target) in enumerate(((n.at[:, pl.ds(1, ROWS)], value_out), (dn, density_out))):
        for r in range(2):
            copies.append(pltpu.make_async_copy(source.at[r], target.at[r], sem.at[2 * k + r]))
    for copy in copies:
        copy.start()
    for copy in copies:
        copy.wait()


def body(value_next, density):
    shape = (2, ROWS, GRID_V, NY)
    haloed = pltpu.VMEM((2, ROWS + 2, GRID_V, NY), F32)
    slab = pltpu.VMEM((ROWS, GRID_V, NY), F32)
    dma = pltpu.SemaphoreType.DMA
    n, dn = pl.pallas_call(
        kernel,
        out_shape=[pltpu.VMEM((2, ROWS + 2, GRID_V, NY), F32), pltpu.VMEM(shape, F32)],
        in_specs=[pl.BlockSpec(memory_space=pltpu.HBM)] * 2,
        out_specs=[pl.BlockSpec(memory_space=pltpu.VMEM)] * 2,
        scratch_shapes=[
            haloed, haloed, slab, slab,
            pltpu.VMEM((VEL, TILE, NY), F32), pltpu.VMEM((2, TILE, NY), F32),
            pltpu.VMEM((len(PASSED), GRID_V, NY), F32),
            dma((2,)), dma((3, 2)), dma((3, 2)), dma((VEL,)), dma((VEL,)),
            dma((2, ROWS + 1)), dma((2, ROWS + 1)), dma((len(PASSED),)), dma((len(PASSED),)),
        ],
        compiler_params=pltpu.CompilerParams(
            collective_id=0, has_side_effects=True, vmem_limit_bytes=52 << 20
        ),
    )(value_next, density)
    return pl.pallas_call(
        store,
        out_shape=[jax.ShapeDtypeStruct(shape, F32)] * 2,
        in_specs=[pl.BlockSpec(memory_space=pltpu.VMEM)] * 2,
        out_specs=[pl.BlockSpec(memory_space=pl.ANY)] * 2,
        scratch_shapes=[dma((4,))],
        compiler_params=pltpu.CompilerParams(vmem_limit_bytes=32 << 20),
    )(n, dn)


def solution(mesh):
    spec = P("pos", "vel", None, None)
    return jax.shard_map(body, mesh=mesh, in_specs=(spec, spec), out_specs=(spec, spec), check_vma=False)
```

time: 67.1 us -> 63.6 us (0.948)
  local copies, waits for them, and re-layouts: 5.71 us -> 0 us
  Pallas kernels: 60.6 us -> 62.9 us
    unnamed x4 -> x0, local copies, waits for them, and re-layouts: 5.71 us -> none
    pallas_call x1 -> x2, Pallas kernels: 60.6 us -> 62.9 us  [the longest x1 59.5 us: body(): pl.pallas_call(kernel, out_shape=[pltpu.VMEM((2, ROWS + 2, GRID_V, NY), F...]
where the time goes in v2:
time: 63.6 us; the launch traced here: 63.5 us
  Pallas kernels  62.9 us (99%)
  between operations  0.64 us (1%)
    pallas_call x1, Pallas kernels, body(): pl.pallas_call(kernel, out_shape=[pltpu.VMEM((2, ROWS + 2, GRID_V, NY), F...  59.5 us
    pallas_call x1, Pallas kernels, body(): pl.pallas_call(store, out_shape=[jax.ShapeDtypeStruct(shape, F32)] * 2, i...  3.37 us

profile of v2, /device:TPU:1, one launch (start us, length us, event | category | flops | bytes accessed | tf_op | source)
XLA Modules:
  0.0 63.5 jit_solution(8908350167035886778)
XLA Ops:
  0.6 59.5 %shard_map.41 = (f32[2,18,64,512]{3,2,1,0:T(8,128)S(1)}, f32[2,16,64,512]{3,2,1,0:T(8,128)S(1)}) custom-call(f32[2,16,64,512]{3,2,1,0:T(8,128)} %value.1, f32[2,16,64,512]{3,2,1,0:T(8,128)} %density.1), custom_call_target="tpu_custom_call" | custom-call | tf_op jit(solution)/shard_map/pallas_call | solution.py:426
  60.1 3.4 %shard_map.42 = (f32[2,16,64,512]{3,2,1,0:T(8,128)}, f32[2,16,64,512]{3,2,1,0:T(8,128)}) custom-call(f32[2,18,64,512]{3,2,1,0:T(8,128)S(1)} %get-tuple-element.4.n, f32[2,16,64,512]{3,2,1,0:T(8,128)S(1)} %get-tuple-element.5.dn), custom_call_target="tpu_custom_call" | custom-call | tf_op jit(solution)/shard_map/pallas_call | solution.py:442

commit v3 on v2

--- a/solution.py
+++ b/solution.py
@@ -18,10 +18,14 @@
 VEL = 4
 POS = 32
 F32 = jnp.float32
-PASSED = range(1, 7)
+ALONG_Y = (1, 2, 3, 4, 5, 6)
+ALONG_Z = (7,)
 
 LAST = ROWS - 2
-ORDER = (1, 2, 3, 0, ROWS - 1, *range(4, ROWS - 1))
+ORDER = (7, 1, 2, 3, 0, ROWS - 1, 4, 5, 6, *range(8, ROWS - 1))
+LATE_ORDER = (0, ROWS - 1, 1, 2, 3, 4, 5, 6, *range(8, ROWS - 1))
+
+FIRST = 10
 
 
 def tile(t):
@@ -102,7 +106,7 @@
 def kernel(
     value, density, n, dn,
     v, d, hv, hd, mass, crowd, passing,
-    load_sem, edge_send, edge_recv, mass_send, mass_recv, x_send, x_recv, pass_send, pass_recv,
+    load_sem, edge_send, edge_recv, mass_send, mass_recv, x_send, x_recv, pass_send, pass_recv, ready,
 ):
     vel, pos = lax.axis_index("vel"), lax.axis_index("pos")
     above, below = lax.rem(pos + 1, POS), lax.rem(pos + POS - 1, POS)
@@ -116,26 +120,60 @@
     place_x = lax.rem(pos, half)
     bottom, top = place_x == 0, place_x == half - 1
     at_end = jnp.logical_or(bottom, top)
+    lower_top, upper_top = pos == half - 1, pos == POS - 1
     twin = lax.rem(pos + half, POS)
     other_end = jnp.where(bottom, pos + half - 1, pos - half + 1)
     high = jnp.logical_not(low)
     value_long = jnp.logical_or(jnp.logical_and(top, low), jnp.logical_and(bottom, high))
     density_long = jnp.logical_and(at_end, jnp.logical_not(value_long))
+    z_steps = (12,)
+    via_z = [jnp.where(bottom, pos + step, pos - step) for step in z_steps]
+    up_helper = [place_x == half - 1 - step for step in z_steps]
+    down_helper = [place_x == step for step in z_steps]
+    helper = [jnp.logical_or(u, w) for u, w in zip(up_helper, down_helper)]
+    helped = [jnp.where(u, pos + step, pos - step) for u, step in zip(up_helper, z_steps)]
+    helped_to = [lax.rem(jnp.where(u, at + 1, at + POS - 1), POS) for u, at in zip(up_helper, helped)]
+    any_up, any_down = up_helper[0], down_helper[0]
+    helps_value = jnp.logical_or(jnp.logical_and(any_up, low), jnp.logical_and(any_down, high))
 
     barrier = pltpu.get_barrier_semaphore()
-    for other in (above, below):
-        pl.semaphore_signal(barrier, inc=1, device_id={"pos": other}, device_id_type=MESH)
+
+    def announce(**device):
+        pl.semaphore_signal(barrier, inc=1, device_id=device, device_id_type=MESH)
+
+    announce(pos=below)
+    pl.when(jnp.logical_not(top))(lambda: announce(pos=above))
     for k in range(1, VEL):
-        pl.semaphore_signal(barrier, inc=1, device_id={"vel": lax.rem(vel + k, VEL)}, device_id_type=MESH)
-
-    @pl.when(at_end)
+        announce(vel=lax.rem(vel + k, VEL))
+
+    @pl.when(bottom)
     def _():
-        pl.semaphore_signal(barrier, inc=1, device_id={"pos": twin}, device_id_type=MESH)
-        pl.semaphore_signal(barrier, inc=1, device_id={"pos": other_end}, device_id_type=MESH)
+        announce(pos=twin)
+        announce(pos=other_end)
+        for step in z_steps:
+            announce(pos=lax.rem(pos + POS - 1 - step, POS))
+
+    pl.when(lower_top)(lambda: announce(pos=twin))
+    for k in range(len(z_steps)):
+        pl.when(helper[k])(lambda: announce(pos=helped[k]))
+        pl.when(down_helper[k])(lambda: announce(pos=helped_to[k]))
 
     load_d = pltpu.make_async_copy(density, d.at[:, pl.ds(1, ROWS)], load_sem.at[0])
     load_v = pltpu.make_async_copy(value, v.at[:, pl.ds(1, ROWS)], load_sem.at[1])
-    pl.semaphore_wait(barrier, jnp.where(at_end, 2 + VEL - 1 + 2, 2 + VEL - 1))
+    expected = jnp.where(bottom, 6, jnp.where(upper_top, 9, jnp.where(top, 8, jnp.where(any_up, 6, 5))))
+    pl.semaphore_wait(barrier, expected)
+
+    def is_ready(**device):
+        pl.semaphore_signal(ready, inc=1, device_id=device, device_id_type=MESH)
+
+    @pl.when(top)
+    def _():
+        is_ready(pos=above)
+        is_ready(pos=other_end)
+        for step in z_steps:
+            is_ready(pos=lax.rem(pos + 1 + step, POS))
+
+    pl.when(upper_top)(lambda: is_ready(pos=twin))
 
     def x_copies(a):
         one = pl.ds(a, 1)
@@ -158,37 +196,73 @@
                 ((value, far, hv, value_to), (density, near, hd, density_to)))
         ]
 
-    def start_x(a):
-        for copy in x_halves(0) + x_halves(1) if a == LAST else x_copies(a):
-            copy.start()
-
-    def start_x_passed(a):
-        one, k = pl.ds(a, 1), a - PASSED[0]
-        for kind, (copy, source, row, crosses) in enumerate(
-            zip(x_copies(a), (value, density), (far, near), (value_long, density_long))
-        ):
-            first_leg = pltpu.make_async_remote_copy(
-                source.at[row, one], passing.at[pl.ds(k, 1)], x_send.at[kind, a], pass_recv.at[k],
-                device_id={"pos": other_end}, device_id_type=MESH)
-            pl.when(crosses)(first_leg.start)
-            pl.when(jnp.logical_not(crosses))(copy.start)
-
-    def second_leg(kind, a):
-        k = a - PASSED[0]
+    def copies_of(a):
+        return x_halves(0) + x_halves(1) if a == LAST else x_copies(a)
+
+    def first_leg(kind, a, to):
+        source = (value.at[far], density.at[near])[kind]
         return pltpu.make_async_remote_copy(
-            passing.at[pl.ds(k, 1)], (hv, hd)[kind].at[pl.ds(a, 1)], pass_send.at[k], x_recv.at[kind, a],
-            device_id={"pos": twin}, device_id_type=MESH)
+            source.at[pl.ds(a, 1)], passing.at[pl.ds(a - 1, 1)], x_send.at[kind, a], pass_recv.at[a - 1],
+            device_id={"pos": to}, device_id_type=MESH)
+
+    def second_leg(kind, a, to):
+        return pltpu.make_async_remote_copy(
+            passing.at[pl.ds(a - 1, 1)], (hv, hd)[kind].at[pl.ds(a, 1)], pass_send.at[a - 1], x_recv.at[kind, a],
+            device_id={"pos": to}, device_id_type=MESH)
+
+    def start_crossing(kind, a):
+        if a in ALONG_Y:
+            first_leg(kind, a, other_end).start()
+        else:
+            for copy in copies_of(a)[kind::2]:
+                copy.start()
+
+    def start_x(rows):
+        @pl.when(jnp.logical_not(at_end))
+        def _():
+            for a in rows:
+                for copy in copies_of(a):
+                    copy.start()
+
+        for kind, crosses in enumerate((value_long, density_long)):
+            @pl.when(jnp.logical_and(at_end, jnp.logical_not(crosses)))
+            def _():
+                for a in rows:
+                    for copy in copies_of(a)[kind::2]:
+                        copy.start()
+
+            @pl.when(crosses)
+            def _():
+                for a in rows:
+                    if a in ALONG_Z:
+                        first_leg(kind, a, via_z[0]).start()
+
+            @pl.when(jnp.logical_and(crosses, top))
+            def _():
+                for a in rows:
+                    if a not in ALONG_Z:
+                        start_crossing(kind, a)
+
+    def start_x_late():
+        for kind, crosses in enumerate((value_long, density_long)):
+            @pl.when(jnp.logical_and(crosses, bottom))
+            def _():
+                for a in LATE_ORDER:
+                    start_crossing(kind, a)
 
     def pass_on(a):
         @pl.when(at_end)
         def _():
-            k = a - PASSED[0]
-            first_leg = pltpu.make_async_remote_copy(
-                value.at[far, pl.ds(a, 1)], passing.at[pl.ds(k, 1)], x_send.at[0, a], pass_recv.at[k],
-                device_id={"pos": other_end}, device_id_type=MESH)
-            first_leg.wait_recv()
-            pl.when(density_long)(lambda: second_leg(0, a).start())
-            pl.when(value_long)(lambda: second_leg(1, a).start())
+            first_leg(0, a, other_end).wait_recv()
+            pl.when(density_long)(lambda: second_leg(0, a, twin).start())
+            pl.when(value_long)(lambda: second_leg(1, a, twin).start())
+
+    def help_on(a):
+        @pl.when(helper[0])
+        def _():
+            first_leg(0, a, helped[0]).wait_recv()
+            pl.when(helps_value)(lambda: second_leg(0, a, helped_to[0]).start())
+            pl.when(jnp.logical_not(helps_value))(lambda: second_leg(1, a, helped_to[0]).start())
 
     def edge_copies(k, source, target):
         to_upper = pltpu.make_async_remote_copy(
@@ -233,14 +307,13 @@
             to_lower.wait_send()
 
     edges_v, edges_d = edge_copies(0, value, v), edge_copies(1, density, d)
-    for a in ORDER:
-        (start_x_passed if a in PASSED else start_x)(a)
-        if a == ORDER[0]:
-            start_pair(edges_v)
-            load_d.start()
-            load_v.start()
-        if a == ORDER[1]:
-            start_pair(edges_d)
+    start_x(ORDER[:1])
+    start_pair(edges_v)
+    load_d.start()
+    load_v.start()
+    start_x(ORDER[1:3])
+    start_pair(edges_d)
+    start_x(ORDER[3:FIRST])
 
     load_d.wait()
     place = sublane()
@@ -266,6 +339,8 @@
     ]
     for copy in mass_copies:
         copy.start()
+    pl.when(bottom)(lambda: pl.semaphore_wait(ready, 2))
+    start_x_late()
     load_v.wait()
 
     def repeat_edges(field, rows):
@@ -317,6 +392,11 @@
     def _(a):
         value_row(far, a, v.at[near, a + 1])
 
+    pl.when(jnp.logical_or(lower_top, any_down))(lambda: pl.semaphore_wait(ready, 1))
+    for a in ALONG_Z:
+        help_on(a)
+    start_x(ORDER[FIRST:])
+
     @pl.loop(2, ROWS - 2)
     def _(a):
         density_row(far, a, None, dn.at[far, a])
@@ -336,9 +416,6 @@
     pass_on(1)
     pass_on(2)
     pass_on(3)
-    pass_on(4)
-    pass_on(5)
-    pass_on(6)
 
     @pl.loop(0, 2)
     def _(i):
@@ -355,6 +432,7 @@
 
     @pl.loop(1, ROWS // 2)
     def _(a):
+        pl.when(a + 3 <= ALONG_Y[-1])(lambda: pass_on(a + 3))
         near_step(a)
 
         @pl.when(a > 1)
@@ -403,8 +481,11 @@
 
     @pl.when(at_end)
     def _():
-        for a in PASSED:
-            second_leg(0, a).wait_send()
+        for a in ALONG_Y:
+            second_leg(0, a, twin).wait_send()
+
+    for a in ALONG_Z:
+        pl.when(helper[0])(lambda: second_leg(0, a, helped_to[0]).wait_send())
 
 
 def store(n, dn, value_out, density_out, sem):
@@ -431,9 +512,9 @@
         scratch_shapes=[
             haloed, haloed, slab, slab,
             pltpu.VMEM((VEL, TILE, NY), F32), pltpu.VMEM((2, TILE, NY), F32),
-            pltpu.VMEM((len(PASSED), GRID_V, NY), F32),
+            pltpu.VMEM((len(ALONG_Y + ALONG_Z), GRID_V, NY), F32),
             dma((2,)), dma((3, 2)), dma((3, 2)), dma((VEL,)), dma((VEL,)),
-            dma((2, ROWS + 1)), dma((2, ROWS + 1)), dma((len(PASSED),)), dma((len(PASSED),)),
+            dma((2, ROWS + 1)), dma((2, ROWS + 1)), dma((len(ALONG_Y + ALONG_Z),)), dma((len(ALONG_Y + ALONG_Z),)), pltpu.SemaphoreType.REGULAR,
         ],
         compiler_params=pltpu.CompilerParams(
             collective_id=0, has_side_effects=True, vmem_limit_bytes=52 << 20

time: 63.6 us -> 60.8 us (0.956)
  Pallas kernels: 62.9 us -> 60.1 us
    pallas_call x1, Pallas kernels: 59.5 us -> 56.7 us  [body(): pl.pallas_call(kernel, out_shape=[pltpu.VMEM((2, ROWS + 2, GRID_V, NY), F...]
where the time goes in v3:
time: 60.8 us; the launch traced here: 60.7 us
  Pallas kernels  60.1 us (99%)
  between operations  0.64 us (1%)
    pallas_call x1, Pallas kernels, body(): pl.pallas_call(kernel, out_shape=[pltpu.VMEM((2, ROWS + 2, GRID_V, NY), F...  56.7 us
    pallas_call x1, Pallas kernels, body(): pl.pallas_call(store, out_shape=[jax.ShapeDtypeStruct(shape, F32)] * 2, i...  3.37 us

profile of v3, /device:TPU:1, one launch (start us, length us, event | category | flops | bytes accessed | tf_op | source)
XLA Modules:
  0.0 60.7 jit_solution(5855493638464633871)
XLA Ops:
  0.6 56.7 %shard_map.41 = (f32[2,18,64,512]{3,2,1,0:T(8,128)S(1)}, f32[2,16,64,512]{3,2,1,0:T(8,128)S(1)}) custom-call(f32[2,16,64,512]{3,2,1,0:T(8,128)} %value.1, f32[2,16,64,512]{3,2,1,0:T(8,128)} %density.1), custom_call_target="tpu_custom_call" | custom-call | tf_op jit(solution)/shard_map/pallas_call | solution.py:507
  57.4 3.4 %shard_map.42 = (f32[2,16,64,512]{3,2,1,0:T(8,128)}, f32[2,16,64,512]{3,2,1,0:T(8,128)}) custom-call(f32[2,18,64,512]{3,2,1,0:T(8,128)S(1)} %get-tuple-element.4.n, f32[2,16,64,512]{3,2,1,0:T(8,128)S(1)} %get-tuple-element.5.dn), custom_call_target="tpu_custom_call" | custom-call | tf_op jit(solution)/shard_map/pallas_call | solution.py:523

commit v4 on v3

--- a/solution.py
+++ b/solution.py
@@ -18,12 +18,14 @@
 VEL = 4
 POS = 32
 F32 = jnp.float32
-ALONG_Y = (1, 2, 3, 4, 5, 6)
-ALONG_Z = (7,)
+ALONG_Y = (1, 2, 3, 4)
+DOWN_Y = (1, 2, 3, 4, 5)
+ALONG_Z = (7, 8)
+NEXT_Z = (7,)
 
 LAST = ROWS - 2
-ORDER = (7, 1, 2, 3, 0, ROWS - 1, 4, 5, 6, *range(8, ROWS - 1))
-LATE_ORDER = (0, ROWS - 1, 1, 2, 3, 4, 5, 6, *range(8, ROWS - 1))
+ORDER = (7, 8, 0, ROWS - 1, 1, 2, 3, 4, 5, 6, *range(9, ROWS - 1))
+LATE_ORDER = (0, ROWS - 1, 1, 2, 3, 4, 5, 6, *range(9, ROWS - 1))
 
 FIRST = 10
 
@@ -126,15 +128,18 @@
     high = jnp.logical_not(low)
     value_long = jnp.logical_or(jnp.logical_and(top, low), jnp.logical_and(bottom, high))
     density_long = jnp.logical_and(at_end, jnp.logical_not(value_long))
-    z_steps = (12,)
-    via_z = [jnp.where(bottom, pos + step, pos - step) for step in z_steps]
-    up_helper = [place_x == half - 1 - step for step in z_steps]
-    down_helper = [place_x == step for step in z_steps]
-    helper = [jnp.logical_or(u, w) for u, w in zip(up_helper, down_helper)]
-    helped = [jnp.where(u, pos + step, pos - step) for u, step in zip(up_helper, z_steps)]
-    helped_to = [lax.rem(jnp.where(u, at + 1, at + POS - 1), POS) for u, at in zip(up_helper, helped)]
-    any_up, any_down = up_helper[0], down_helper[0]
-    helps_value = jnp.logical_or(jnp.logical_and(any_up, low), jnp.logical_and(any_down, high))
+    up_1, down_1 = place_x == 3, place_x == 12
+    up_2, down_2 = place_x == 7, place_x == 8
+    any_1, any_2 = jnp.logical_or(up_1, down_1), jnp.logical_or(up_2, down_2)
+    helper = jnp.logical_or(any_1, any_2)
+    any_up = jnp.logical_or(up_1, up_2)
+    reach = jnp.where(any_2, -4, 12)
+    helped = jnp.where(any_up, pos + reach, pos - reach)
+    helped_to = lax.rem(jnp.where(any_up, helped + 1, helped + POS - 1), POS)
+    helps_value = jnp.logical_and(helper, jnp.where(any_up, low, high))
+    via_z = jnp.where(bottom, pos + 12, jnp.where(top, pos - 12, jnp.where(up_1, pos + 4, pos - 4)))
+    value_next_z = jnp.logical_and(any_1, helps_value)
+    density_next_z = jnp.logical_and(any_1, jnp.logical_not(helps_value))
 
     barrier = pltpu.get_barrier_semaphore()
 
@@ -150,17 +155,16 @@
     def _():
         announce(pos=twin)
         announce(pos=other_end)
-        for step in z_steps:
-            announce(pos=lax.rem(pos + POS - 1 - step, POS))
 
     pl.when(lower_top)(lambda: announce(pos=twin))
-    for k in range(len(z_steps)):
-        pl.when(helper[k])(lambda: announce(pos=helped[k]))
-        pl.when(down_helper[k])(lambda: announce(pos=helped_to[k]))
+    pl.when(helper)(lambda: announce(pos=helped))
+    pl.when(any_1)(lambda: announce(pos=helped_to))
+    pl.when(place_x == 4)(lambda: announce(pos=pos + 3))
+    pl.when(place_x == 11)(lambda: announce(pos=pos - 3))
 
     load_d = pltpu.make_async_copy(density, d.at[:, pl.ds(1, ROWS)], load_sem.at[0])
     load_v = pltpu.make_async_copy(value, v.at[:, pl.ds(1, ROWS)], load_sem.at[1])
-    expected = jnp.where(bottom, 6, jnp.where(upper_top, 9, jnp.where(top, 8, jnp.where(any_up, 6, 5))))
+    expected = jnp.where(bottom, 7, jnp.where(upper_top, 9, jnp.where(top, 8, jnp.where(helper, 6, 5))))
     pl.semaphore_wait(barrier, expected)
 
     def is_ready(**device):
@@ -170,10 +174,10 @@
     def _():
         is_ready(pos=above)
         is_ready(pos=other_end)
-        for step in z_steps:
-            is_ready(pos=lax.rem(pos + 1 + step, POS))
+        is_ready(pos=lax.rem(pos + 13, POS))
 
     pl.when(upper_top)(lambda: is_ready(pos=twin))
+    pl.when(bottom)(lambda: is_ready(pos=lax.rem(pos + POS - 13, POS)))
 
     def x_copies(a):
         one = pl.ds(a, 1)
@@ -210,32 +214,43 @@
             passing.at[pl.ds(a - 1, 1)], (hv, hd)[kind].at[pl.ds(a, 1)], pass_send.at[a - 1], x_recv.at[kind, a],
             device_id={"pos": to}, device_id_type=MESH)
 
-    def start_crossing(kind, a):
-        if a in ALONG_Y:
+    def start_crossing(kind, a, passed=ALONG_Y):
+        if a in passed:
             first_leg(kind, a, other_end).start()
         else:
             for copy in copies_of(a)[kind::2]:
                 copy.start()
 
+    special = jnp.logical_or(at_end, any_1)
+
     def start_x(rows):
-        @pl.when(jnp.logical_not(at_end))
+        @pl.when(jnp.logical_not(special))
         def _():
             for a in rows:
                 for copy in copies_of(a):
                     copy.start()
 
-        for kind, crosses in enumerate((value_long, density_long)):
-            @pl.when(jnp.logical_and(at_end, jnp.logical_not(crosses)))
+        for kind, (crosses, turns) in enumerate(((value_long, value_next_z), (density_long, density_next_z))):
+            @pl.when(jnp.logical_and(special, jnp.logical_not(jnp.logical_or(crosses, turns))))
             def _():
                 for a in rows:
                     for copy in copies_of(a)[kind::2]:
                         copy.start()
 
+            @pl.when(turns)
+            def _():
+                for a in rows:
+                    if a in NEXT_Z:
+                        first_leg(kind, a, via_z).start()
+                    else:
+                        for copy in copies_of(a)[kind::2]:
+                            copy.start()
+
             @pl.when(crosses)
             def _():
                 for a in rows:
                     if a in ALONG_Z:
-                        first_leg(kind, a, via_z[0]).start()
+                        first_leg(kind, a, via_z).start()
 
             @pl.when(jnp.logical_and(crosses, top))
             def _():
@@ -248,21 +263,24 @@
             @pl.when(jnp.logical_and(crosses, bottom))
             def _():
                 for a in LATE_ORDER:
-                    start_crossing(kind, a)
-
-    def pass_on(a):
-        @pl.when(at_end)
+                    start_crossing(kind, a, DOWN_Y)
+
+    def pass_on(a, where=at_end):
+        @pl.when(where)
         def _():
             first_leg(0, a, other_end).wait_recv()
             pl.when(density_long)(lambda: second_leg(0, a, twin).start())
             pl.when(value_long)(lambda: second_leg(1, a, twin).start())
 
+    def helps_with(a):
+        return helper if a in NEXT_Z else any_1
+
     def help_on(a):
-        @pl.when(helper[0])
-        def _():
-            first_leg(0, a, helped[0]).wait_recv()
-            pl.when(helps_value)(lambda: second_leg(0, a, helped_to[0]).start())
-            pl.when(jnp.logical_not(helps_value))(lambda: second_leg(1, a, helped_to[0]).start())
+        @pl.when(helps_with(a))
+        def _():
+            first_leg(0, a, helped).wait_recv()
+            pl.when(helps_value)(lambda: second_leg(0, a, helped_to).start())
+            pl.when(jnp.logical_not(helps_value))(lambda: second_leg(1, a, helped_to).start())
 
     def edge_copies(k, source, target):
         to_upper = pltpu.make_async_remote_copy(
@@ -388,18 +406,12 @@
     def near_density(a, **tiles):
         density_row(near, a, d.at[far, a + 1], dn.at[near, a], **tiles)
 
-    @pl.loop(1, ROWS - 1)
-    def _(a):
-        value_row(far, a, v.at[near, a + 1])
-
-    pl.when(jnp.logical_or(lower_top, any_down))(lambda: pl.semaphore_wait(ready, 1))
-    for a in ALONG_Z:
-        help_on(a)
-    start_x(ORDER[FIRST:])
-
-    @pl.loop(2, ROWS - 2)
-    def _(a):
-        density_row(far, a, None, dn.at[far, a])
+    def inner_values(here):
+        @pl.loop(jnp.where(here, 1, ROWS - 1), ROWS - 1)
+        def _(a):
+            value_row(far, a, v.at[near, a + 1])
+
+    inner_values(at_end)
 
     receive_pair(edges_v)
 
@@ -413,13 +425,17 @@
     edges_n = edge_copies(2, n.at[:, pl.ds(1, ROWS)], n)
     start_pair(edges_n)
     repeat_edges(n, (0, 1))
+    inner_values(jnp.logical_not(at_end))
+    pl.when(jnp.logical_or(lower_top, any_1))(lambda: pl.semaphore_wait(ready, 1))
+    for a in ALONG_Z:
+        help_on(a)
+    start_x(ORDER[FIRST:])
     pass_on(1)
     pass_on(2)
     pass_on(3)
 
-    @pl.loop(0, 2)
-    def _(i):
-        a = 1 + i * (ROWS - 3)
+    @pl.loop(1, ROWS - 1)
+    def _(a):
         density_row(far, a, None, dn.at[far, a])
 
     receive_pair(edges_d)
@@ -433,6 +449,7 @@
     @pl.loop(1, ROWS // 2)
     def _(a):
         pl.when(a + 3 <= ALONG_Y[-1])(lambda: pass_on(a + 3))
+        pl.when(a + 3 == DOWN_Y[-1])(lambda: pass_on(a + 3, top))
         near_step(a)
 
         @pl.when(a > 1)
@@ -484,8 +501,10 @@
         for a in ALONG_Y:
             second_leg(0, a, twin).wait_send()
 
+    pl.when(top)(lambda: second_leg(0, DOWN_Y[-1], twin).wait_send())
+
     for a in ALONG_Z:
-        pl.when(helper[0])(lambda: second_leg(0, a, helped_to[0]).wait_send())
+        pl.when(helps_with(a))(lambda: second_leg(0, a, helped_to).wait_send())
 
 
 def store(n, dn, value_out, density_out, sem):
@@ -512,9 +531,9 @@
         scratch_shapes=[
             haloed, haloed, slab, slab,
             pltpu.VMEM((VEL, TILE, NY), F32), pltpu.VMEM((2, TILE, NY), F32),
-            pltpu.VMEM((len(ALONG_Y + ALONG_Z), GRID_V, NY), F32),
+            pltpu.VMEM((ALONG_Z[-1], GRID_V, NY), F32),
             dma((2,)), dma((3, 2)), dma((3, 2)), dma((VEL,)), dma((VEL,)),
-            dma((2, ROWS + 1)), dma((2, ROWS + 1)), dma((len(ALONG_Y + ALONG_Z),)), dma((len(ALONG_Y + ALONG_Z),)), pltpu.SemaphoreType.REGULAR,
+            dma((2, ROWS + 1)), dma((2, ROWS + 1)), dma((ALONG_Z[-1],)), dma((ALONG_Z[-1],)), pltpu.SemaphoreType.REGULAR,
         ],
         compiler_params=pltpu.CompilerParams(
             collective_id=0, has_side_effects=True, vmem_limit_bytes=52 << 20

time: 60.8 us -> 58.7 us (0.965)
  Pallas kernels: 60.1 us -> 57.4 us
    pallas_call x1, Pallas kernels: 56.7 us -> 54 us  [body(): pl.pallas_call(kernel, out_shape=[pltpu.VMEM((2, ROWS + 2, GRID_V, NY), F...]
where the time goes in v4:
time: 58.7 us; the launch traced here: 58 us
  Pallas kernels  57.4 us (98%)
  between operations  0.64 us (1%)
    pallas_call x1, Pallas kernels, body(): pl.pallas_call(kernel, out_shape=[pltpu.VMEM((2, ROWS + 2, GRID_V, NY), F...  54 us
    pallas_call x1, Pallas kernels, body(): pl.pallas_call(store, out_shape=[jax.ShapeDtypeStruct(shape, F32)] * 2, i...  3.37 us

profile of v4, /device:TPU:1, one launch (start us, length us, event | category | flops | bytes accessed | tf_op | source)
XLA Modules:
  0.0 58.0 jit_solution(5489436256515209649)
XLA Ops:
  0.6 54.0 %shard_map.41 = (f32[2,18,64,512]{3,2,1,0:T(8,128)S(1)}, f32[2,16,64,512]{3,2,1,0:T(8,128)S(1)}) custom-call(f32[2,16,64,512]{3,2,1,0:T(8,128)} %value.1, f32[2,16,64,512]{3,2,1,0:T(8,128)} %density.1), custom_call_target="tpu_custom_call" | custom-call | tf_op jit(solution)/shard_map/pallas_call | solution.py:526
  54.7 3.4 %shard_map.42 = (f32[2,16,64,512]{3,2,1,0:T(8,128)}, f32[2,16,64,512]{3,2,1,0:T(8,128)}) custom-call(f32[2,18,64,512]{3,2,1,0:T(8,128)S(1)} %get-tuple-element.4.n, f32[2,16,64,512]{3,2,1,0:T(8,128)S(1)} %get-tuple-element.5.dn), custom_call_target="tpu_custom_call" | custom-call | tf_op jit(solution)/shard_map/pallas_call | solution.py:542

commit v5 on v4

--- a/solution.py
+++ b/solution.py
@@ -106,8 +106,8 @@
 
 
 def kernel(
-    value, density, n, dn,
-    v, d, hv, hd, mass, crowd, passing,
+    value, density, n, dn, v, d, hv, hd, crowd,
+    mass, passing,
     load_sem, edge_send, edge_recv, mass_send, mass_recv, x_send, x_recv, pass_send, pass_recv, ready,
 ):
     vel, pos = lax.axis_index("vel"), lax.axis_index("pos")
@@ -471,17 +471,8 @@
         near_step(a)
         near_density(a - 1)
 
-    middle = TILES // 2
-    for half, (first, stop, inner_first, inner_stop) in enumerate(
-        ((0, middle, 0, middle - 1), (middle, TILES, middle - 1, TILES))
-    ):
-        for copy in x_halves(half):
-            copy.wait_recv()
-        value_row(near, LAST, hv.at[LAST], first=first, stop=stop)
-        finish_far(LAST, first, stop)
-        near_density(LAST - 1, first=first, stop=stop)
-        near_density(LAST, first=inner_first, stop=inner_stop)
-        near_density(LAST + 1, first=first, stop=stop)
+    for copy in x_halves(0) + x_halves(1):
+        copy.wait_recv()
 
     for pair in (edges_v, edges_d, edges_n):
         sent_pair(pair)
@@ -507,15 +498,50 @@
         pl.when(helps_with(a))(lambda: second_leg(0, a, helped_to).wait_send())
 
 
-def store(n, dn, value_out, density_out, sem):
-    copies = []
-    for k, (source, target) in enumerate(((n.at[:, pl.ds(1, ROWS)], value_out), (dn, density_out))):
-        for r in range(2):
-            copies.append(pltpu.make_async_copy(source.at[r], target.at[r], sem.at[2 * k + r]))
-    for copy in copies:
-        copy.start()
-    for copy in copies:
-        copy.wait()
+def store(n, dn, v, d, hv, hd, crowd, value_out, density_out, last_value, last_density, last_far, sem):
+    vel = lax.axis_index("vel")
+    near = jnp.where(vel < VEL // 2, 0, 1)
+    far = 1 - near
+    count = [0]
+
+    def copy(source, target):
+        made = pltpu.make_async_copy(source, target, sem.at[count[0]])
+        count[0] += 1
+        made.start()
+        return made
+
+    def rows(first, stop):
+        return pl.ds(first, stop - first)
+
+    copies = [
+        copy(n.at[far, rows(1, ROWS + 1)], value_out.at[far]),
+        copy(n.at[near, rows(1, LAST + 1)], value_out.at[near, rows(0, LAST)]),
+        copy(dn.at[far, rows(0, LAST)], density_out.at[far, rows(0, LAST)]),
+        copy(dn.at[near, rows(0, LAST - 1)], density_out.at[near, rows(0, LAST - 1)]),
+        copy(n.at[near, rows(LAST + 2, ROWS + 1)], value_out.at[near, rows(LAST + 1, ROWS)]),
+        copy(dn.at[far, rows(LAST + 1, ROWS)], density_out.at[far, rows(LAST + 1, ROWS)]),
+    ]
+
+    def speed(a):
+        index = (vel * ROWS + a).astype(F32)
+        return jnp.abs(COURANT * ((index + 0.5 - GRID_V / 2) / (GRID_V / 2)))
+
+    for t in range(TILES):
+        last_far[0, tile(t), :] = dn[far, LAST, tile(t), :] + speed(LAST) * hd[LAST, tile(t), :]
+    copies.append(copy(last_far, density_out.at[far, rows(LAST, LAST + 1)]))
+    at = LAST + 1
+    value_slab(
+        v.at[near, at], v.at[near, at + 1], v.at[near, at - 1], hv.at[LAST], crowd[near], speed(LAST), last_value.at[0])
+    copies.append(copy(last_value, value_out.at[near, rows(LAST, LAST + 1)]))
+    levels = [n.at[near, at - 2], n.at[near, at - 1], last_value.at[0], n.at[near, at + 1], n.at[near, at + 2]]
+    for k in range(3):
+        here = at - 1 + k
+        density_slab(
+            levels[k + 1], levels[k + 2], levels[k], d.at[near, here], d.at[near, here + 1], d.at[near, here - 1],
+            d.at[far, here], speed(here - 1), last_density.at[k])
+    copies.append(copy(last_density, density_out.at[near, rows(LAST - 1, ROWS)]))
+    for made in copies:
+        made.wait()
 
 
 def body(value_next, density):
@@ -523,30 +549,29 @@
     haloed = pltpu.VMEM((2, ROWS + 2, GRID_V, NY), F32)
     slab = pltpu.VMEM((ROWS, GRID_V, NY), F32)
     dma = pltpu.SemaphoreType.DMA
-    n, dn = pl.pallas_call(
+    held = pl.pallas_call(
         kernel,
-        out_shape=[pltpu.VMEM((2, ROWS + 2, GRID_V, NY), F32), pltpu.VMEM(shape, F32)],
+        out_shape=[haloed, pltpu.VMEM(shape, F32), haloed, haloed, slab, slab, pltpu.VMEM((2, TILE, NY), F32)],
         in_specs=[pl.BlockSpec(memory_space=pltpu.HBM)] * 2,
-        out_specs=[pl.BlockSpec(memory_space=pltpu.VMEM)] * 2,
+        out_specs=[pl.BlockSpec(memory_space=pltpu.VMEM)] * 7,
         scratch_shapes=[
-            haloed, haloed, slab, slab,
-            pltpu.VMEM((VEL, TILE, NY), F32), pltpu.VMEM((2, TILE, NY), F32),
+            pltpu.VMEM((VEL, TILE, NY), F32),
             pltpu.VMEM((ALONG_Z[-1], GRID_V, NY), F32),
             dma((2,)), dma((3, 2)), dma((3, 2)), dma((VEL,)), dma((VEL,)),
             dma((2, ROWS + 1)), dma((2, ROWS + 1)), dma((ALONG_Z[-1],)), dma((ALONG_Z[-1],)), pltpu.SemaphoreType.REGULAR,
         ],
         compiler_params=pltpu.CompilerParams(
-            collective_id=0, has_side_effects=True, vmem_limit_bytes=52 << 20
+            collective_id=0, has_side_effects=True, vmem_limit_bytes=40 << 20
         ),
     )(value_next, density)
     return pl.pallas_call(
         store,
         out_shape=[jax.ShapeDtypeStruct(shape, F32)] * 2,
-        in_specs=[pl.BlockSpec(memory_space=pltpu.VMEM)] * 2,
+        in_specs=[pl.BlockSpec(memory_space=pltpu.VMEM)] * 7,
         out_specs=[pl.BlockSpec(memory_space=pl.ANY)] * 2,
-        scratch_shapes=[dma((4,))],
-        compiler_params=pltpu.CompilerParams(vmem_limit_bytes=32 << 20),
-    )(n, dn)
+        scratch_shapes=[pltpu.VMEM((1, GRID_V, NY), F32), pltpu.VMEM((3, GRID_V, NY), F32), pltpu.VMEM((1, GRID_V, NY), F32), dma((9,))],
+        compiler_params=pltpu.CompilerParams(vmem_limit_bytes=8 << 20),
+    )(*held)
 
 
 def solution(mesh):

time: 58.7 us -> 58.5 us (level)
  no operation moved by 1% of the time
where the time goes in v5:
time: 58.5 us; the launch traced here: 57.9 us
  Pallas kernels  57.2 us (98%)
  between operations  0.64 us (1%)
    pallas_call x1, Pallas kernels, body(): pl.pallas_call(kernel, out_shape=[haloed, pltpu.VMEM(shape, F32), haloed,...  53.7 us
    pallas_call x1, Pallas kernels, body(): pl.pallas_call(store, out_shape=[jax.ShapeDtypeStruct(shape, F32)] * 2, i...  3.56 us

profile of v5, /device:TPU:1, one launch (start us, length us, event | category | flops | bytes accessed | tf_op | source)
XLA Modules:
  0.0 57.9 jit_solution(9076934372405229221)
XLA Ops:
  0.6 53.7 %shard_map.41 = (f32[2,18,64,512]{3,2,1,0:T(8,128)S(1)}, f32[2,16,64,512]{3,2,1,0:T(8,128)S(1)}, f32[2,18,64,512]{3,2,1,0:T(8,128)S(1)}, f32[2,18,64,512]{3,2,1,...) custom-call(f32[2,16,64,512]{3,2,1,0:T(8,128)} %value.1, ...), custom_call_target="tpu_custom_call" | custom-call | tf_op jit(solution)/shard_map/pallas_call | solution.py:552
  54.3 3.6 %shard_map.42 = (f32[2,16,64,512]{3,2,1,0:T(8,128)}, f32[2,16,64,512]{3,2,1,0:T(8,128)}) custom-call(f32[2,18,64,512]{3,2,1,0:T(8,128)S(1)} %get-tuple-element.9.n, f32[2,16,64,512]{3,2,1,0:T(8,128)S(1)} %get-tuple-element.10.dn, f32[2,18,64,512]{3,2,1,0:T(8,128)S(1)} %get-tuple-element.11.v, f32[2,18,64,512]{3,2,1,0:T(8,128)S(1)} %get-tuple-element.12.d, ...), custom_call_target="tpu_custom_call" | custom-call | tf_op jit(solution)/shard_map/pallas_call | solution.py:567

commit v6 on v5

--- a/solution.py
+++ b/solution.py
@@ -27,7 +27,7 @@
 ORDER = (7, 8, 0, ROWS - 1, 1, 2, 3, 4, 5, 6, *range(9, ROWS - 1))
 LATE_ORDER = (0, ROWS - 1, 1, 2, 3, 4, 5, 6, *range(9, ROWS - 1))
 
-FIRST = 10
+FIRST = 12
 
 
 def tile(t):

time: 58.5 us -> 58.5 us (level)
  no operation moved by 1% of the time
where the time goes in v6:
time: 58.5 us; the launch traced here: 57.9 us
  Pallas kernels  57.2 us (98%)
  between operations  0.64 us (1%)
    pallas_call x1, Pallas kernels, body(): pl.pallas_call(kernel, out_shape=[haloed, pltpu.VMEM(shape, F32), haloed,...  53.7 us
    pallas_call x1, Pallas kernels, body(): pl.pallas_call(store, out_shape=[jax.ShapeDtypeStruct(shape, F32)] * 2, i...  3.56 us

profile of v6, /device:TPU:1, one launch (start us, length us, event | category | flops | bytes accessed | tf_op | source)
XLA Modules:
  0.0 57.9 jit_solution(18367182497378287693)
XLA Ops:
  0.6 53.7 %shard_map.41 = (f32[2,18,64,512]{3,2,1,0:T(8,128)S(1)}, f32[2,16,64,512]{3,2,1,0:T(8,128)S(1)}, f32[2,18,64,512]{3,2,1,0:T(8,128)S(1)}, f32[2,18,64,512]{3,2,1,...) custom-call(f32[2,16,64,512]{3,2,1,0:T(8,128)} %value.1, ...), custom_call_target="tpu_custom_call" | custom-call | tf_op jit(solution)/shard_map/pallas_call | solution.py:552
  54.3 3.6 %shard_map.42 = (f32[2,16,64,512]{3,2,1,0:T(8,128)}, f32[2,16,64,512]{3,2,1,0:T(8,128)}) custom-call(f32[2,18,64,512]{3,2,1,0:T(8,128)S(1)} %get-tuple-element.9.n, f32[2,16,64,512]{3,2,1,0:T(8,128)S(1)} %get-tuple-element.10.dn, f32[2,18,64,512]{3,2,1,0:T(8,128)S(1)} %get-tuple-element.11.v, f32[2,18,64,512]{3,2,1,0:T(8,128)S(1)} %get-tuple-element.12.d, ...), custom_call_target="tpu_custom_call" | custom-call | tf_op jit(solution)/shard_map/pallas_call | solution.py:567

commit v7 on v6

--- a/solution.py
+++ b/solution.py
@@ -325,11 +325,11 @@
             to_lower.wait_send()
 
     edges_v, edges_d = edge_copies(0, value, v), edge_copies(1, density, d)
-    start_x(ORDER[:1])
+    start_x(ORDER[:2])
     start_pair(edges_v)
     load_d.start()
     load_v.start()
-    start_x(ORDER[1:3])
+    start_x(ORDER[2:3])
     start_pair(edges_d)
     start_x(ORDER[3:FIRST])
 

time: 58.5 us -> 58.5 us (level)
  no operation moved by 1% of the time
where the time goes in v7:
time: 58.5 us; the launch traced here: 57.9 us
  Pallas kernels  57.2 us (98%)
  between operations  0.64 us (1%)
    pallas_call x1, Pallas kernels, body(): pl.pallas_call(kernel, out_shape=[haloed, pltpu.VMEM(shape, F32), haloed,...  53.7 us
    pallas_call x1, Pallas kernels, body(): pl.pallas_call(store, out_shape=[jax.ShapeDtypeStruct(shape, F32)] * 2, i...  3.56 us

profile of v7, /device:TPU:1, one launch (start us, length us, event | category | flops | bytes accessed | tf_op | source)
XLA Modules:
  0.0 57.9 jit_solution(13556153020386898152)
XLA Ops:
  0.6 53.7 %shard_map.41 = (f32[2,18,64,512]{3,2,1,0:T(8,128)S(1)}, f32[2,16,64,512]{3,2,1,0:T(8,128)S(1)}, f32[2,18,64,512]{3,2,1,0:T(8,128)S(1)}, f32[2,18,64,512]{3,2,1,...) custom-call(f32[2,16,64,512]{3,2,1,0:T(8,128)} %value.1, ...), custom_call_target="tpu_custom_call" | custom-call | tf_op jit(solution)/shard_map/pallas_call | solution.py:552
  54.3 3.6 %shard_map.42 = (f32[2,16,64,512]{3,2,1,0:T(8,128)}, f32[2,16,64,512]{3,2,1,0:T(8,128)}) custom-call(f32[2,18,64,512]{3,2,1,0:T(8,128)S(1)} %get-tuple-element.9.n, f32[2,16,64,512]{3,2,1,0:T(8,128)S(1)} %get-tuple-element.10.dn, f32[2,18,64,512]{3,2,1,0:T(8,128)S(1)} %get-tuple-element.11.v, f32[2,18,64,512]{3,2,1,0:T(8,128)S(1)} %get-tuple-element.12.d, ...), custom_call_target="tpu_custom_call" | custom-call | tf_op jit(solution)/shard_map/pallas_call | solution.py:567
